TPU v7x, 512 devices: a whole 4x8x8 slice. The times are simulated.
512 devices in a mesh: gx: 8 (over z), gy: 8 (over y), gz: 8 (over x, core).
Axes of the slice: x: 4, y: 8, z: 8, core: 2. Of those that a mesh axis runs over, the one named last changes fastest.
Arguments:
- source_term: float32 [128, 256, 1024], P('gx', 'gy', 'gz'), may hold values from -4 to 4
- conductivity: float32 [128, 256, 1024], P('gx', 'gy', 'gz'), may hold values from 0.5 to 8
Outputs:
- solution: float32 [128, 256, 1024], P('gx', 'gy', 'gz')
All inputs are finite; a program needn't handle non-finite values.
Results may differ from a plain program's by a relative error of at most 0.0003.
Values sent between devices are 32-bit elements; how exact they have to be, the bound alone decides.
A program may use at most 128 MiB of HBM per device.

v0:
```python
import jax
import jax.numpy as jnp
from jax import lax
from jax.sharding import PartitionSpec as P

SWEEPS = 2
BOTTOM = 16


def extended(value, sides, width):
    for axis, dim in sides:
        devices, length = (lax.axis_size(axis), value.shape[dim])
        up = [(i, (i + 1) % devices) for i in range(devices - 1)]
        down = [(j, i) for i, j in up]
        last = lax.slice_in_dim(value, length - width, length, axis=dim)
        initial = lax.slice_in_dim(value, 0, width, axis=dim)
        before = lax.ppermute(last, axis, up)
        after = lax.ppermute(initial, axis, down)
        value = jnp.concatenate([before, value, after], axis=dim)
    return value


def coefficients(padded, factor):
    centre = padded[1:-1, 1:-1, 1:-1]
    lower_x = factor * 0.5 * (centre + padded[:-2, 1:-1, 1:-1])
    upper_x = factor * 0.5 * (centre + padded[2:, 1:-1, 1:-1])
    lower_y = factor * 0.5 * (centre + padded[1:-1, :-2, 1:-1])
    upper_y = factor * 0.5 * (centre + padded[1:-1, 2:, 1:-1])
    lower_z = factor * 0.5 * (centre + padded[1:-1, 1:-1, :-2])
    upper_z = factor * 0.5 * (centre + padded[1:-1, 1:-1, 2:])
    diagonal = lower_x + upper_x + lower_y + upper_y + lower_z + upper_z
    return (lower_x, upper_x, lower_y, upper_y, lower_z, upper_z, diagonal)


def neighbours(stencil, padded):
    summed = stencil[0] * padded[:-2, 1:-1, 1:-1] + stencil[1] * padded[2:, 1:-1, 1:-1]
    summed = summed + stencil[2] * padded[1:-1, :-2, 1:-1] + stencil[3] * padded[1:-1, 2:, 1:-1]
    summed = summed + stencil[4] * padded[1:-1, 1:-1, :-2] + stencil[5] * padded[1:-1, 1:-1, 2:]
    return summed


def coarsen(values):
    size_x, size_y, size_z = values.shape
    blocks = values.reshape(size_x // 2, 2, size_y // 2, 2, size_z // 2, 2)
    return jnp.mean(blocks, axis=(1, 3, 5))


def prolong(values):
    return jnp.repeat(jnp.repeat(jnp.repeat(values, 2, axis=0), 2, axis=1), 2, axis=2)


def parity(extent, starts, margin):
    summed = jnp.zeros(extent, jnp.int32)
    for axis_no in range(3):
        summed = (
            summed + lax.broadcasted_iota(jnp.int32, extent, axis_no) + (starts[axis_no] - margin)
        )
    return summed % 2 == 0


def pad_zero(values, width):
    return jnp.pad(values, width)


def pad_all(values, width):
    return extended(values, (("gx", 0), ("gy", 1), ("gz", 2)), width)


def pad_yz(values, width):
    inner = extended(values, (("gy", 1), ("gz", 2)), width)
    return jnp.pad(inner, ((width, width), (0, 0), (0, 0)))


def pad_z(values, width):
    inner = extended(values, (("gz", 2),), width)
    return jnp.pad(inner, ((width, width), (width, width), (0, 0)))


def join_x(values):
    return lax.all_gather(values, "gx", axis=0, tiled=True)


def join_y(values):
    return lax.all_gather(values, "gy", axis=1, tiled=True)


def join_z(values):
    return lax.all_gather(values, "gz", axis=2, tiled=True)


def relaxation(iterate, source, stencil, red_cells, padder):
    for colour_mask in (red_cells, jnp.logical_not(red_cells)):
        padded = padder(iterate, 1)
        updated = (source + neighbours(stencil, padded)) / stencil[6]
        iterate = jnp.where(colour_mask, updated, iterate)
    return iterate


def prepare(conduct_grid, padder, starts, factor):
    red_cells = parity(conduct_grid.shape, starts, 0)
    stencil = coefficients(padder(conduct_grid, 1), factor)
    return (stencil, stencil, red_cells, red_cells)


def smooth(iterate, source, level_data, padder):
    stencil, stencil_circle, red_cells, red_circle = level_data
    for sweep_no in range(SWEEPS):
        iterate = relaxation(iterate, source, stencil, red_cells, padder)
    return iterate


def on_device(source_term, conductivity):
    cells_x, cells_y, cells_z = source_term.shape
    index_x = lax.axis_index("gx")
    index_y = lax.axis_index("gy")
    index_z = lax.axis_index("gz")
    zero_start = jnp.int32(0)
    starts = [
        (index_x * cells_x, index_y * cells_y, index_z * cells_z),
        (index_x * (cells_x // 2), index_y * (cells_y // 2), index_z * (cells_z // 2)),
        (zero_start, index_y * (cells_y // 4), index_z * (cells_z // 4)),
        (zero_start, zero_start, index_z * (cells_z // 8)),
        (zero_start, zero_start, zero_start),
    ]
    padders = [pad_all, pad_all, pad_yz, pad_z, pad_zero]
    conduct_levels = [conductivity, coarsen(conductivity)]
    conduct_levels.append(join_x(coarsen(conduct_levels[1])))
    conduct_levels.append(join_y(coarsen(conduct_levels[2])))
    conduct_levels.append(join_z(coarsen(conduct_levels[3])))
    level_data = []
    for level_no in range(5):
        level_data.append(
            prepare(conduct_levels[level_no], padders[level_no], starts[level_no], 0.25**level_no)
        )
    sources = [source_term]
    circles = []
    states = []
    for level_no in range(4):
        source = sources[level_no]
        padder = padders[level_no]
        circles.append(source)
        iterate = smooth(jnp.zeros_like(source), source, level_data[level_no], padder)
        stencil = level_data[level_no][0]
        residual = source - (stencil[6] * iterate - neighbours(stencil, padder(iterate, 1)))
        states.append(iterate)
        coarse = coarsen(residual)
        if level_no == 1:
            coarse = join_x(coarse)
        elif level_no == 2:
            coarse = join_y(coarse)
        elif level_no == 3:
            coarse = join_z(coarse)
        sources.append(coarse)
    bottom = level_data[4]

    def bottom_sweep(sweep_no, current):
        return relaxation(current, sources[4], bottom[0], bottom[2], pad_zero)

    iterate = lax.fori_loop(0, BOTTOM, bottom_sweep, jnp.zeros_like(sources[4]))
    for level_no in (3, 2, 1, 0):
        coarse = iterate
        if level_no == 3:
            coarse = lax.dynamic_slice_in_dim(coarse, index_z * (cells_z // 16), cells_z // 16, 2)
        elif level_no == 2:
            coarse = lax.dynamic_slice_in_dim(coarse, index_y * (cells_y // 8), cells_y // 8, 1)
        elif level_no == 1:
            coarse = lax.dynamic_slice_in_dim(coarse, index_x * (cells_x // 4), cells_x // 4, 0)
        iterate = states[level_no] + prolong(coarse)
        iterate = smooth(iterate, sources[level_no], level_data[level_no], padders[level_no])
    return iterate


def solution(mesh):
    in_specs = (P("gx", "gy", "gz"), P("gx", "gy", "gz"))
    out_specs = P("gx", "gy", "gz")
    return jax.shard_map(
        on_device, mesh=mesh, in_specs=in_specs, out_specs=out_specs, check_vma=False
    )
```

profile of v0, /device:TPU:1, one launch (start us, length us, event | category | flops | bytes accessed | tf_op | source)
XLA Modules:
  0.0 1298.7 jit_solution(9540463776765444631)
XLA Ops:
  0.0 4.8 collective-permute-start.1
  13.4 4.6 collective-permute-start
  18.1 18.9 %reshape.62 = f32[8,2,16,2,64,2]{5,4,3,2,1,0:T(8,128)} reshape(f32[16,32,128]{2,1,0:T(8,128)} %param.5) | data formatting | bytes 524288 | tf_op jit(solution)/shard_map/reshape | solution.py:44
  36.9 7.1 reduce_sum.73
  89.0 6.6 fusion.122
  96.6 5.8 collective-permute-start.12
  104.4 5.5 collective-permute-start.36
  114.5 4.9 collective-permute-start.14
  122.3 5.0 collective-permute-start.16
  146.0 6.0 fusion.120
  153.0 4.9 collective-permute-start.18
  170.3 4.6 collective-permute-start.20
  204.5 6.0 fusion.110
  212.2 5.5 collective-permute-start.24
  227.7 5.8 collective-permute-start.26
  260.5 6.0 fusion.100
  268.1 4.8 collective-permute-start.30
  282.6 5.5 collective-permute-start.32
  288.8 4.8 collective-permute-start.45
  316.4 6.6 fusion.90
  325.2 18.9 %reshape.61 = f32[8,2,16,2,64,2]{5,4,3,2,1,0:T(8,128)} reshape(f32[16,32,128]{2,1,0:T(8,128)} %copy.509) | data formatting | bytes 524288 | tf_op jit(solution)/shard_map/reshape | solution.py:44
  344.1 7.1 reduce_sum.72
  352.7 5.1 collective-permute-start.48
  371.9 5.3 collective-permute-start.52
  388.8 5.4 collective-permute-start.76
  416.3 21.6 %all_gather.19 = f32[32,8,32]{2,1,0:T(8,128)} all-gather(f32[4,8,32]{2,1,0:T(8,128)S(1)} %broadcast_multiply_fusion.3), channel_id=1, replica_groups=mesh['gx'=8,'gy'=8,'gz'=8] {'gx'}, dimensions={0}, use_global_device_ids=true | all-gather | bytes 36864 | tf_op jit(solution)/shard_map/all_gather | solution.py:80
  457.6 10.9 collective-permute-start.74
  493.8 4.7 collective-permute-start.68
  503.6 5.9 collective-permute-start.70
  524.0 21.1 %all_gather.18 = f32[32,8,32]{2,1,0:T(8,128)} all-gather(f32[4,8,32]{2,1,0:T(8,128)S(1)} %broadcast_multiply_fusion.4), channel_id=1, replica_groups=mesh['gx'=8,'gy'=8,'gz'=8] {'gx'}, dimensions={0}, use_global_device_ids=true | all-gather | bytes 36864 | tf_op jit(solution)/shard_map/all_gather | solution.py:80
  558.1 8.4 collective-permute-start.82
  583.3 4.8 collective-permute-start.84
  593.6 4.8 collective-permute-start.86
  600.3 20.6 %all_gather.21 = f32[16,32,16]{2,0,1:T(8,128)} all-gather(f32[16,4,16]{2,0,1:T(8,128)S(1)} %copy_multiply_fusion), channel_id=1, replica_groups=mesh['gx'=8,'gy'=8,'gz'=8] {'gy'}, dimensions={1}, use_global_device_ids=true | all-gather | bytes 36864 | tf_op jit(solution)/shard_map/all_gather | solution.py:84
  633.0 10.1 collective-permute-start.96
  684.5 20.8 %all_gather.20 = f32[16,32,16]{2,0,1:T(8,128)} all-gather(f32[16,4,16]{2,0,1:T(8,128)S(1)} %copy_multiply_fusion.1), channel_id=1, replica_groups=mesh['gx'=8,'gy'=8,'gz'=8] {'gy'}, dimensions={1}, use_global_device_ids=true | all-gather | bytes 36864 | tf_op jit(solution)/shard_map/all_gather | solution.py:84
  710.1 8.2 collective-permute-start.100
  744.0 12.7 all_gather.22
  786.3 13.6 %all_gather.23 = f32[8,16,64]{1,0,2:T(8,128)} all-gather(f32[8,16,8]{1,0,2:T(8,128)S(1)} %copy.548), channel_id=1, replica_groups=mesh['gx'=8,'gy'=8,'gz'=8] {'gz'}, dimensions={2}, use_global_device_ids=true | all-gather | bytes 36864 | tf_op jit(solution)/shard_map/all_gather | solution.py:88
  801.6 60.2 %while.14 = (s32[]{:T(128)}, f32[8,16,64]{2,1,0:T(8,128)}, f32[8,16,64]{2,1,0:T(8,128)}, f32[8,16,64]{2,1,0:T(8,128)}, f32[8,16,64]{2,1,0:T(8,128)}, /*index=5*/...) while((s32[]{:T(128)}, f32[8,16,64]{2,1,0:T(8,128)}, ...), condition=%wide.region_9.10_spmd.clone.clone, body=%wide.region_8.9_spmd.clone.clone.sunk | while | flops 466947 | bytes 721023 | solution.py:159
  1000.0 4.7 collective-permute-start.132
  1016.5 4.8 collective-permute-start.136
  1070.0 4.6 collective-permute-start.148
  1128.2 4.7 collective-permute-start.160
  1150.4 6.0 fusion.81
  1196.7 6.0 fusion.71
  1243.0 6.0 fusion.61
  1289.0 7.0 fusion.51
  (922 shorter events, 917.0 us)
Async XLA Ops:
  0.0 45.9 %collective-permute-start.1 = (f32[1,32,128]{1,0,2:T(1,128)S(1)}, f32[1,32,128]{1,0,2:T(1,128)S(1)}, u32[]{:S(2)}, u32[]{:S(2)}) collective-permute-start(f32[1,32,128]{1,0,2:T(1,128)S(1)} %broadcast.147), channel_id=1, source_target_pairs={{0,64},{64,128},{128,192},{192,256},{256,320},{320,384},{384,448},... | collective-permute-start | bytes 49160 | tf_op jit(solution)/shard_map/ppermute | solution.py:17
  4.9 42.4 %collective-permute-start.3 = (f32[1,32,128]{1,0,2:T(1,128)S(1)}, f32[1,32,128]{1,0,2:T(1,128)S(1)}, u32[]{:S(2)}, u32[]{:S(2)}) collective-permute-start(f32[1,32,128]{1,0,2:T(1,128)S(1)} %broadcast.147), channel_id=1, source_target_pairs={{64,0},{128,64},{192,128},{256,192},{320,256},{384,320},{448,384},... | collective-permute-start | bytes 49160 | tf_op jit(solution)/shard_map/ppermute | solution.py:18
  6.8 163.6 %collective-permute-start.37 = (f32[1,16,64]{2,1,0:T(8,128)}, f32[1,16,64]{2,1,0:T(8,128)S(1)}, u32[]{:S(2)}, u32[]{:S(2)}) collective-permute-start(f32[1,16,64]{2,1,0:T(8,128)} %broadcast.150), channel_id=1, source_target_pairs={{0,64},{64,128},{128,192},{192,256},{256,320},{320,384},{384,448},... | collective-permute-start | bytes 12296 | tf_op jit(solution)/shard_map/ppermute | solution.py:17
  11.4 163.6 %collective-permute-start.39 = (f32[1,16,64]{2,1,0:T(8,128)}, f32[1,16,64]{2,1,0:T(8,128)S(1)}, u32[]{:S(2)}, u32[]{:S(2)}) collective-permute-start(f32[1,16,64]{2,1,0:T(8,128)} %broadcast.150), channel_id=1, source_target_pairs={{64,0},{128,64},{192,128},{256,192},{320,256},{384,320},{448,384},... | collective-permute-start | bytes 12296 | tf_op jit(solution)/shard_map/ppermute | solution.py:18
  13.4 35.3 %collective-permute-start = (f32[1,32,128]{2,1,0:T(8,128)S(1)}, f32[1,32,128]{2,1,0:T(8,128)S(1)}, u32[]{:S(2)}, u32[]{:S(2)}) collective-permute-start(f32[1,32,128]{2,1,0:T(8,128)S(1)} %get-tuple-element.380), channel_id=1, source_target_pairs={{0,64},{64,128},{128,192},{192,256},{256,320},{320,384},{384,448},... | collective-permute-start | bytes 49160 | tf_op jit(solution)/shard_map/ppermute | solution.py:17
  47.5 11.5 collective-permute-start.7
  52.9 12.7 collective-permute-start.4
  61.3 11.9 collective-permute-start.11
  69.6 12.5 collective-permute-start.10
  96.6 15.5 %collective-permute-start.12 = (f32[1,32,128]{1,0,2:T(1,128)S(1)}, f32[1,32,128]{1,0,2:T(1,128)S(1)}, u32[]{:S(2)}, u32[]{:S(2)}) collective-permute-start(f32[1,32,128]{1,0,2:T(1,128)S(1)} %get-tuple-element.302), channel_id=1, source_target_pairs={{0,64},{64,128},{128,192},{192,256},{256,320},{320,384},{384,448},... | collective-permute-start | bytes 49160 | tf_op jit(solution)/shard_map/ppermute | solution.py:17
  104.4 53.4 %collective-permute-start.36 = (f32[1,16,64]{2,1,0:T(8,128)}, f32[1,16,64]{2,1,0:T(8,128)S(1)}, u32[]{:S(2)}, u32[]{:S(2)}) collective-permute-start(f32[1,16,64]{2,1,0:T(8,128)} %get-tuple-element.498), channel_id=1, source_target_pairs={{0,64},{64,128},{128,192},{192,256},{256,320},{320,384},{384,448},... | collective-permute-start | bytes 12296 | tf_op jit(solution)/shard_map/ppermute | solution.py:17
  132.3 26.9 %collective-permute-start.38 = (f32[1,16,64]{2,1,0:T(8,128)}, f32[1,16,64]{2,1,0:T(8,128)S(1)}, u32[]{:S(2)}, u32[]{:S(2)}) collective-permute-start(f32[1,16,64]{2,1,0:T(8,128)} %get-tuple-element.497), channel_id=1, source_target_pairs={{64,0},{128,64},{192,128},{256,192},{320,256},{384,320},{448,384},... | collective-permute-start | bytes 12296 | tf_op jit(solution)/shard_map/ppermute | solution.py:18
  153.0 13.7 %collective-permute-start.18 = (f32[1,32,128]{1,0,2:T(1,128)S(1)}, f32[1,32,128]{1,0,2:T(1,128)S(1)}, u32[]{:S(2)}, u32[]{:S(2)}) collective-permute-start(f32[1,32,128]{1,0,2:T(1,128)S(1)} %get-tuple-element.300), channel_id=1, source_target_pairs={{0,64},{64,128},{128,192},{192,256},{256,320},{320,384},{384,448},... | collective-permute-start | bytes 49160 | tf_op jit(solution)/shard_map/ppermute | solution.py:17
  159.8 57.9 %collective-permute-start.40 = (f32[10,1,64]{2,1,0:T(1,128)}, f32[10,1,64]{2,1,0:T(1,128)}, u32[]{:S(2)}, u32[]{:S(2)}) collective-permute-start(f32[10,1,64]{2,1,0:T(1,128)} %get-tuple-element.478), channel_id=1, source_target_pairs={{0,8},{8,16},{16,24},{24,32},{32,40},{40,48},{48,56},{1,9},{9,17},... | collective-permute-start | bytes 7688 | tf_op jit(solution)/shard_map/ppermute | solution.py:17
  166.7 52.3 %collective-permute-start.42 = (f32[10,1,64]{2,1,0:T(1,128)}, f32[10,1,64]{2,1,0:T(1,128)S(1)}, u32[]{:S(2)}, u32[]{:S(2)}) collective-permute-start(f32[10,1,64]{2,1,0:T(1,128)} %get-tuple-element.477), channel_id=1, source_target_pairs={{8,0},{16,8},{24,16},{32,24},{40,32},{48,40},{56,48},{9,1},{17,9},... | collective-permute-start | bytes 7688 | tf_op jit(solution)/shard_map/ppermute | solution.py:18
  175.6 97.4 %collective-permute-start.41 = (f32[10,1,64]{2,1,0:T(1,128)}, f32[10,1,64]{2,1,0:T(1,128)S(1)}, u32[]{:S(2)}, u32[]{:S(2)}) collective-permute-start(f32[10,1,64]{2,1,0:T(1,128)} %get-tuple-element.479), channel_id=1, source_target_pairs={{0,8},{8,16},{16,24},{24,32},{32,40},{40,48},{48,56},{1,9},{9,17},... | collective-permute-start | bytes 7688 | tf_op jit(solution)/shard_map/ppermute | solution.py:17
  190.8 84.0 %collective-permute-start.43 = (f32[10,1,64]{2,1,0:T(1,128)}, f32[10,1,64]{2,1,0:T(1,128)}, u32[]{:S(2)}, u32[]{:S(2)}) collective-permute-start(f32[10,1,64]{2,1,0:T(1,128)} %get-tuple-element.480), channel_id=1, source_target_pairs={{8,0},{16,8},{24,16},{32,24},{40,32},{48,40},{56,48},{9,1},{17,9},... | collective-permute-start | bytes 7688 | tf_op jit(solution)/shard_map/ppermute | solution.py:18
  234.2 117.0 %collective-permute-start.44 = (f32[10,18,1]{2,1,0:T(8,128)}, f32[10,18,1]{2,1,0:T(8,128)}, u32[]{:S(2)}, u32[]{:S(2)}) collective-permute-start(f32[10,18,1]{2,1,0:T(8,128)} %get-tuple-element.458), channel_id=1, source_target_pairs={{0,1},{1,2},{2,3},{3,4},{4,5},{5,6},{6,7},{8,9},{9,10},{10,11},{11... | collective-permute-start | bytes 2168 | tf_op jit(solution)/shard_map/ppermute | solution.py:17
  247.9 103.3 %collective-permute-start.46 = (f32[10,18,1]{2,1,0:T(8,128)}, f32[10,18,1]{2,1,0:T(8,128)}, u32[]{:S(2)}, u32[]{:S(2)}) collective-permute-start(f32[10,18,1]{2,1,0:T(8,128)} %get-tuple-element.457), channel_id=1, source_target_pairs={{1,0},{2,1},{3,2},{4,3},{5,4},{6,5},{7,6},{9,8},{10,9},{11,10},{12... | collective-permute-start | bytes 2168 | tf_op jit(solution)/shard_map/ppermute | solution.py:18
  281.3 12.3 collective-permute-start.33
  288.8 62.4 %collective-permute-start.45 = (f32[10,18,1]{2,1,0:T(8,128)}, f32[10,18,1]{2,1,0:T(8,128)}, u32[]{:S(2)}, u32[]{:S(2)}) collective-permute-start(f32[10,18,1]{2,1,0:T(8,128)} %get-tuple-element.459), channel_id=1, source_target_pairs={{0,1},{1,2},{2,3},{3,4},{4,5},{5,6},{6,7},{8,9},{9,10},{10,11},{11... | collective-permute-start | bytes 2168 | tf_op jit(solution)/shard_map/ppermute | solution.py:17
  303.9 47.3 %collective-permute-start.47 = (f32[10,18,1]{2,1,0:T(8,128)}, f32[10,18,1]{2,1,0:T(8,128)}, u32[]{:S(2)}, u32[]{:S(2)}) collective-permute-start(f32[10,18,1]{2,1,0:T(8,128)} %get-tuple-element.460), channel_id=1, source_target_pairs={{1,0},{2,1},{3,2},{4,3},{5,4},{6,5},{7,6},{9,8},{10,9},{11,10},{12... | collective-permute-start | bytes 2168 | tf_op jit(solution)/shard_map/ppermute | solution.py:18
  383.5 17.5 %collective-permute-start.54 = (f32[1,16,64]{2,1,0:T(8,128)S(1)}, f32[1,16,64]{2,1,0:T(8,128)S(1)}, u32[]{:S(2)}, u32[]{:S(2)}) collective-permute-start(f32[1,16,64]{2,1,0:T(8,128)S(1)} %get-tuple-element.493), channel_id=1, source_target_pairs={{0,64},{64,128},{128,192},{192,256},{256,320},{320,384},{384,448},... | collective-permute-start | bytes 12296 | tf_op jit(solution)/shard_map/ppermute | solution.py:17
  386.9 14.1 %collective-permute-start.55 = (f32[1,16,64]{2,1,0:T(8,128)S(1)}, f32[1,16,64]{2,1,0:T(8,128)S(1)}, u32[]{:S(2)}, u32[]{:S(2)}) collective-permute-start(f32[1,16,64]{2,1,0:T(8,128)S(1)} %get-tuple-element.494), channel_id=1, source_target_pairs={{64,0},{128,64},{192,128},{256,192},{320,256},{384,320},{448,384},... | collective-permute-start | bytes 12296 | tf_op jit(solution)/shard_map/ppermute | solution.py:18
  388.8 86.4 %collective-permute-start.76 = (f32[32,1,32]{0,1,2:T(1,128)}, f32[32,1,32]{0,1,2:T(1,128)}, u32[]{:S(2)}, u32[]{:S(2)}) collective-permute-start(f32[32,1,32]{0,1,2:T(1,128)} %broadcast.155), channel_id=1, source_target_pairs={{0,8},{8,16},{16,24},{24,32},{32,40},{40,48},{48,56},{1,9},{9,17},... | collective-permute-start | bytes 12296 | tf_op jit(solution)/shard_map/ppermute | solution.py:17
  394.2 82.9 %collective-permute-start.77 = (f32[32,1,32]{0,1,2:T(1,128)}, f32[32,1,32]{0,1,2:T(1,128)}, u32[]{:S(2)}, u32[]{:S(2)}) collective-permute-start(f32[32,1,32]{0,1,2:T(1,128)} %broadcast.155), channel_id=1, source_target_pairs={{8,0},{16,8},{24,16},{32,24},{40,32},{48,40},{56,48},{9,1},{17,9},... | collective-permute-start | bytes 12296 | tf_op jit(solution)/shard_map/ppermute | solution.py:18
  410.8 28.1 %collective-permute-start.58 = (f32[10,18,1]{2,1,0:T(8,128)}, f32[10,18,1]{2,1,0:T(8,128)}, u32[]{:S(2)}, u32[]{:S(2)}) collective-permute-start(f32[10,18,1]{2,1,0:T(8,128)} %get-tuple-element.453), channel_id=1, source_target_pairs={{0,1},{1,2},{2,3},{3,4},{4,5},{5,6},{6,7},{8,9},{9,10},{10,11},{11... | collective-permute-start | bytes 2168 | tf_op jit(solution)/shard_map/ppermute | solution.py:17
  414.3 24.6 %collective-permute-start.59 = (f32[10,18,1]{2,1,0:T(8,128)}, f32[10,18,1]{2,1,0:T(8,128)}, u32[]{:S(2)}, u32[]{:S(2)}) collective-permute-start(f32[10,18,1]{2,1,0:T(8,128)} %get-tuple-element.454), channel_id=1, source_target_pairs={{1,0},{2,1},{3,2},{4,3},{5,4},{6,5},{7,6},{9,8},{10,9},{11,10},{12... | collective-permute-start | bytes 2168 | tf_op jit(solution)/shard_map/ppermute | solution.py:18
  452.0 16.5 %collective-permute-start.62 = (f32[10,1,64]{2,1,0:T(1,128)S(1)}, f32[10,1,64]{2,1,0:T(1,128)S(1)}, u32[]{:S(2)}, u32[]{:S(2)}) collective-permute-start(f32[10,1,64]{2,1,0:T(1,128)S(1)} %get-tuple-element.471), channel_id=1, source_target_pairs={{0,8},{8,16},{16,24},{24,32},{32,40},{40,48},{48,56},{1,9},{9,17},... | collective-permute-start | bytes 7688 | tf_op jit(solution)/shard_map/ppermute | solution.py:17
  456.2 14.2 %collective-permute-start.63 = (f32[10,1,64]{2,1,0:T(1,128)S(1)}, f32[10,1,64]{2,1,0:T(1,128)S(1)}, u32[]{:S(2)}, u32[]{:S(2)}) collective-permute-start(f32[10,1,64]{2,1,0:T(1,128)S(1)} %get-tuple-element.472), channel_id=1, source_target_pairs={{8,0},{16,8},{24,16},{32,24},{40,32},{48,40},{56,48},{9,1},{17,9},... | collective-permute-start | bytes 7688 | tf_op jit(solution)/shard_map/ppermute | solution.py:18
  457.6 31.8 %collective-permute-start.74 = (f32[32,10,1]{0,1,2:T(8,128)S(1)}, f32[32,10,1]{0,1,2:T(8,128)S(1)}, u32[]{:S(2)}, u32[]{:S(2)}) collective-permute-start(f32[32,10,1]{0,1,2:T(8,128)S(1)} %get-tuple-element.403), channel_id=1, source_target_pairs={{0,1},{1,2},{2,3},{3,4},{4,5},{5,6},{6,7},{8,9},{9,10},{10,11},{11... | collective-permute-start | bytes 3848 | tf_op jit(solution)/shard_map/ppermute | solution.py:17
  468.5 22.2 %collective-permute-start.75 = (f32[32,10,1]{0,1,2:T(8,128)S(1)}, f32[32,10,1]{0,1,2:T(8,128)S(1)}, u32[]{:S(2)}, u32[]{:S(2)}) collective-permute-start(f32[32,10,1]{0,1,2:T(8,128)S(1)} %get-tuple-element.404), channel_id=1, source_target_pairs={{1,0},{2,1},{3,2},{4,3},{5,4},{6,5},{7,6},{9,8},{10,9},{11,10},{12... | collective-permute-start | bytes 3848 | tf_op jit(solution)/shard_map/ppermute | solution.py:18
  477.9 33.6 %collective-permute-start.78 = (f32[32,10,1]{0,1,2:T(8,128)S(1)}, f32[32,10,1]{0,1,2:T(8,128)S(1)}, u32[]{:S(2)}, u32[]{:S(2)}) collective-permute-start(f32[32,10,1]{0,1,2:T(8,128)S(1)} %get-tuple-element.401), channel_id=1, source_target_pairs={{0,1},{1,2},{2,3},{3,4},{4,5},{5,6},{6,7},{8,9},{9,10},{10,11},{11... | collective-permute-start | bytes 3848 | tf_op jit(solution)/shard_map/ppermute | solution.py:17
  481.5 30.0 %collective-permute-start.79 = (f32[32,10,1]{0,1,2:T(8,128)S(1)}, f32[32,10,1]{0,1,2:T(8,128)S(1)}, u32[]{:S(2)}, u32[]{:S(2)}) collective-permute-start(f32[32,10,1]{0,1,2:T(8,128)S(1)} %get-tuple-element.402), channel_id=1, source_target_pairs={{1,0},{2,1},{3,2},{4,3},{5,4},{6,5},{7,6},{9,8},{10,9},{11,10},{12... | collective-permute-start | bytes 3848 | tf_op jit(solution)/shard_map/ppermute | solution.py:18
  558.1 22.2 %collective-permute-start.82 = (f32[32,10,1]{0,1,2:T(8,128)}, f32[32,10,1]{0,1,2:T(8,128)}, u32[]{:S(2)}, u32[]{:S(2)}) collective-permute-start(f32[32,10,1]{0,1,2:T(8,128)} %get-tuple-element.399), channel_id=1, source_target_pairs={{0,1},{1,2},{2,3},{3,4},{4,5},{5,6},{6,7},{8,9},{9,10},{10,11},{11... | collective-permute-start | bytes 3848 | tf_op jit(solution)/shard_map/ppermute | solution.py:17
  566.4 13.8 %collective-permute-start.83 = (f32[32,10,1]{0,1,2:T(8,128)}, f32[32,10,1]{0,1,2:T(8,128)}, u32[]{:S(2)}, u32[]{:S(2)}) collective-permute-start(f32[32,10,1]{0,1,2:T(8,128)} %get-tuple-element.400), channel_id=1, source_target_pairs={{1,0},{2,1},{3,2},{4,3},{5,4},{6,5},{7,6},{9,8},{10,9},{11,10},{12... | collective-permute-start | bytes 3848 | tf_op jit(solution)/shard_map/ppermute | solution.py:18
  568.9 103.2 %collective-permute-start.98 = (f32[16,32,1]{1,0,2:T(8,128)}, f32[16,32,1]{1,0,2:T(8,128)}, u32[]{:S(2)}, u32[]{:S(2)}) collective-permute-start(f32[16,32,1]{1,0,2:T(8,128)} %broadcast.159), channel_id=1, source_target_pairs={{0,1},{1,2},{2,3},{3,4},{4,5},{5,6},{6,7},{8,9},{9,10},{10,11},{11... | collective-permute-start | bytes 6152 | tf_op jit(solution)/shard_map/ppermute | solution.py:17
  572.6 99.6 %collective-permute-start.99 = (f32[16,32,1]{1,0,2:T(8,128)}, f32[16,32,1]{1,0,2:T(8,128)}, u32[]{:S(2)}, u32[]{:S(2)}) collective-permute-start(f32[16,32,1]{1,0,2:T(8,128)} %broadcast.159), channel_id=1, source_target_pairs={{1,0},{2,1},{3,2},{4,3},{5,4},{6,5},{7,6},{9,8},{10,9},{11,10},{12... | collective-permute-start | bytes 6152 | tf_op jit(solution)/shard_map/ppermute | solution.py:18
  593.6 29.1 %collective-permute-start.86 = (f32[32,10,1]{0,1,2:T(8,128)}, f32[32,10,1]{0,1,2:T(8,128)}, u32[]{:S(2)}, u32[]{:S(2)}) collective-permute-start(f32[32,10,1]{0,1,2:T(8,128)} %get-tuple-element.397), channel_id=1, source_target_pairs={{0,1},{1,2},{2,3},{3,4},{4,5},{5,6},{6,7},{8,9},{9,10},{10,11},{11... | collective-permute-start | bytes 3848 | tf_op jit(solution)/shard_map/ppermute | solution.py:17
  598.4 24.3 %collective-permute-start.87 = (f32[32,10,1]{0,1,2:T(8,128)}, f32[32,10,1]{0,1,2:T(8,128)}, u32[]{:S(2)}, u32[]{:S(2)}) collective-permute-start(f32[32,10,1]{0,1,2:T(8,128)} %get-tuple-element.398), channel_id=1, source_target_pairs={{1,0},{2,1},{3,2},{4,3},{5,4},{6,5},{7,6},{9,8},{10,9},{11,10},{12... | collective-permute-start | bytes 3848 | tf_op jit(solution)/shard_map/ppermute | solution.py:18
  627.0 16.1 %collective-permute-start.88 = (f32[32,1,32]{0,1,2:T(1,128)}, f32[32,1,32]{0,1,2:T(1,128)}, u32[]{:S(2)}, u32[]{:S(2)}) collective-permute-start(f32[32,1,32]{0,1,2:T(1,128)} %get-tuple-element.433), channel_id=1, source_target_pairs={{0,8},{8,16},{16,24},{24,32},{32,40},{40,48},{48,56},{1,9},{9,17},... | collective-permute-start | bytes 12296 | tf_op jit(solution)/shard_map/ppermute | solution.py:17
  630.4 14.8 %collective-permute-start.89 = (f32[32,1,32]{0,1,2:T(1,128)}, f32[32,1,32]{0,1,2:T(1,128)}, u32[]{:S(2)}, u32[]{:S(2)}) collective-permute-start(f32[32,1,32]{0,1,2:T(1,128)} %get-tuple-element.434), channel_id=1, source_target_pairs={{8,0},{16,8},{24,16},{32,24},{40,32},{48,40},{56,48},{9,1},{17,9},... | collective-permute-start | bytes 12296 | tf_op jit(solution)/shard_map/ppermute | solution.py:18
  633.0 16.6 %collective-permute-start.96 = (f32[16,32,1]{1,0,2:T(8,128)}, f32[16,32,1]{1,0,2:T(8,128)}, u32[]{:S(2)}, u32[]{:S(2)}) collective-permute-start(f32[16,32,1]{1,0,2:T(8,128)} %get-tuple-element.429), channel_id=1, source_target_pairs={{0,1},{1,2},{2,3},{3,4},{4,5},{5,6},{6,7},{8,9},{9,10},{10,11},{11... | collective-permute-start | bytes 6152 | tf_op jit(solution)/shard_map/ppermute | solution.py:17
  710.1 17.7 %collective-permute-start.100 = (f32[16,32,1]{1,0,2:T(8,128)}, f32[16,32,1]{1,0,2:T(8,128)}, u32[]{:S(2)}, u32[]{:S(2)}) collective-permute-start(f32[16,32,1]{1,0,2:T(8,128)} %get-tuple-element.427), channel_id=1, source_target_pairs={{0,1},{1,2},{2,3},{3,4},{4,5},{5,6},{6,7},{8,9},{9,10},{10,11},{11... | collective-permute-start | bytes 6152 | tf_op jit(solution)/shard_map/ppermute | solution.py:17
  739.6 17.0 %collective-permute-start.104 = (f32[16,32,1]{1,0,2:T(8,128)S(1)}, f32[16,32,1]{1,0,2:T(8,128)S(1)}, u32[]{:S(2)}, u32[]{:S(2)}) collective-permute-start(f32[16,32,1]{1,0,2:T(8,128)S(1)} %get-tuple-element.423), channel_id=1, source_target_pairs={{0,1},{1,2},{2,3},{3,4},{4,5},{5,6},{6,7},{8,9},{9,10},{10,11},{11... | collective-permute-start | bytes 6152 | tf_op jit(solution)/shard_map/ppermute | solution.py:17
  741.6 15.1 %collective-permute-start.105 = (f32[16,32,1]{1,0,2:T(8,128)S(1)}, f32[16,32,1]{1,0,2:T(8,128)S(1)}, u32[]{:S(2)}, u32[]{:S(2)}) collective-permute-start(f32[16,32,1]{1,0,2:T(8,128)S(1)} %get-tuple-element.424), channel_id=1, source_target_pairs={{1,0},{2,1},{3,2},{4,3},{5,4},{6,5},{7,6},{9,8},{10,9},{11,10},{12... | collective-permute-start | bytes 6152 | tf_op jit(solution)/shard_map/ppermute | solution.py:18
  758.3 18.2 %collective-permute-start.106 = (f32[16,32,1]{1,0,2:T(8,128)}, f32[16,32,1]{1,0,2:T(8,128)}, u32[]{:S(2)}, u32[]{:S(2)}) collective-permute-start(f32[16,32,1]{1,0,2:T(8,128)} %get-tuple-element.421), channel_id=1, source_target_pairs={{0,1},{1,2},{2,3},{3,4},{4,5},{5,6},{6,7},{8,9},{9,10},{10,11},{11... | collective-permute-start | bytes 6152 | tf_op jit(solution)/shard_map/ppermute | solution.py:17
  761.0 15.6 %collective-permute-start.107 = (f32[16,32,1]{1,0,2:T(8,128)}, f32[16,32,1]{1,0,2:T(8,128)}, u32[]{:S(2)}, u32[]{:S(2)}) collective-permute-start(f32[16,32,1]{1,0,2:T(8,128)} %get-tuple-element.422), channel_id=1, source_target_pairs={{1,0},{2,1},{3,2},{4,3},{5,4},{6,5},{7,6},{9,8},{10,9},{11,10},{12... | collective-permute-start | bytes 6152 | tf_op jit(solution)/shard_map/ppermute | solution.py:18
  (240 other events, 4312.1 us)
where the time goes:
time: 1320 us; the launch traced here: 1300 us
  starting transfers between devices  525 us (40%)
  local copies, waits for them, and re-layouts  257 us (19%)
  other arithmetic  247 us (19%)
  waiting for transfers between devices  155 us (12%)
  blocking collectives  110 us (8%)
    ppermute x90, starting transfers between devices, extended(): before = lax.ppermute(last, axis, up)  373 us
    ppermute x90, waiting for transfers between devices, extended(): after = lax.ppermute(initial, axis, down)  151 us
    ppermute x90, starting transfers between devices, extended(): after = lax.ppermute(initial, axis, down)  151 us
    select_n x64, other arithmetic, relaxation(): iterate = jnp.where(colour_mask, updated, iterate)  121 us
    unnamed x269, local copies, waits for them, and re-layouts  112 us
    reshape x7, local copies, waits for them, and re-layouts, coarsen(): blocks = values.reshape(size_x // 2, 2, size_y // 2, 2, size_z // 2, 2)  55.3 us
    concatenate x62, other arithmetic, extended(): value = jnp.concatenate([before, value, after], axis=dim)  50.8 us
    all_gather x2, blocking collectives, join_x(): return lax.all_gather(values, 'gx', axis=0, tiled=True)  42.7 us
  transfers between devices with their start and end apart: 180, of which 56 were waited for; matrix products, arithmetic and copies ran while one was open for 21% of the time, Pallas kernels for 0%

commit v1 on v0

v1 whole, which is shorter than its diff:
```python
import functools

import jax
import jax.numpy as jnp
from jax import lax
from jax.experimental import pallas as pl
from jax.experimental.pallas import tpu as pltpu
from jax.sharding import PartitionSpec as P

MESH = pl.DeviceIdType.MESH
AXES = ("gx", "gy", "gz")
N = 8
BOTTOM = 16
F32 = jnp.float32


def iota(shape, axis):
    return lax.broadcasted_iota(jnp.int32, shape, axis)


def dot(a, b):
    return lax.dot_general(
        a, b, (((1,), (0,)), ((), ())),
        precision=lax.Precision.HIGHEST, preferred_element_type=F32,
    )


def rotate(a, shift, axis):
    shift = shift % a.shape[axis]
    return a if shift == 0 else pltpu.roll(a, shift, axis)


class Level:
    def __init__(self, refs, h, scale, closed):
        (self.f, self.k, self.wx, self.wy, self.wz, self.ir, self.ib, self.d, self.ur, self.ub) = refs
        self.planes, self.rows, self.lanes = self.ur.shape
        self.h, self.scale, self.closed = (h, scale, closed)

    def prepare(self, lo, hi):
        shape = (self.rows, self.lanes)
        hs = 0.5 * self.scale

        def body(p, carry):
            k = self.k[p]
            below, above = self.k[p - 1], self.k[p + 1]
            kyl, kyu = rotate(k, 1, 0), rotate(k, -1, 0)
            kzl, kzu = rotate(k, 1, 1), rotate(k, -1, 1)
            wy, wz = hs * (k + kyl), hs * (k + kzl)
            if self.closed:
                row, lane = iota(shape, 0), iota(shape, 1)
                kyl = jnp.where(row == 0, 0.0, kyl)
                kyu = jnp.where(row == self.rows - 1, 0.0, kyu)
                kzl = jnp.where(lane == 0, 0.0, kzl)
                kzu = jnp.where(lane == self.lanes - 1, 0.0, kzu)
                wy = jnp.where(row == 0, 0.0, wy)
                wz = jnp.where(lane == 0, 0.0, wz)
            diag = hs * (6.0 * k + below + above + kyl + kyu + kzl + kzu)
            inside = k > 0.0
            inv = jnp.where(inside, 1.0 / jnp.where(inside, diag, 1.0), 0.0)
            odd = (iota(shape, 0) + iota(shape, 1) + (p - self.h)) & 1
            red = jnp.where(odd == 0, inv, 0.0)
            self.wx[p] = hs * (k + below)
            self.wy[p] = wy
            self.wz[p] = wz
            self.ir[p] = red
            self.ib[p] = inv - red
            self.d[p] = diag
            return carry

        lax.fori_loop(lo, hi, body, 0)
        self.wx[hi] = hs * (self.k[hi] + self.k[hi - 1])

    def around(self, plane, p):
        u, wy, wz = plane(p), self.wy[p], self.wz[p]
        total = self.wx[p] * plane(p - 1) + self.wx[p + 1] * plane(p + 1)
        total = total + (wy * rotate(u, 1, 0) + rotate(wy * u, -1, 0))
        return total + (wz * rotate(u, 1, 1) + rotate(wz * u, -1, 1))

    def first(self, lo, hi):
        def body(p, carry):
            self.ur[p] = self.ir[p] * self.f[p]
            return carry

        lax.fori_loop(lo, hi, body, 0)

    def half(self, target, inverse, other, lo, hi):
        def body(p, carry):
            target[p] = inverse[p] * (self.f[p] + self.around(lambda q: other[q], p))
            return carry

        lax.fori_loop(lo, hi, body, 0, unroll=2)

    def red(self, lo, hi, black):
        self.half(self.ur, self.ir, black, lo, hi)

    def black(self, lo, hi, black):
        self.half(black, self.ib, self.ur, lo, hi)

    def residual_pairs(self, first, count, rows, out):
        def one(p):
            u = self.ur[p] + self.ub[p]
            applied = self.d[p] * u - self.around(lambda q: self.ur[q] + self.ub[q], p)
            return (self.f[p] - applied)[rows[0] : rows[1], 0:128]

        def body(i, carry):
            out[i] = one(first + 2 * i) + one(first + 2 * i + 1)
            return carry

        lax.fori_loop(0, count, body, 0)


def row_pairs(ref, count):
    return ref[pl.ds(0, count, 2), :] + ref[pl.ds(1, count, 2), :]


def kernel(f_hbm, k_hbm, out_ref, *scratch):
    names = list(SCRATCH)
    s = dict(zip(names, scratch))
    ix, iy, iz = (lax.axis_index(a) for a in AXES)
    me = (ix, iy, iz)

    def device(off):
        return tuple(lax.rem(me[a] + (off[a] + N), N) for a in range(3))

    send, recv, dummy = s["send"], s["recv"], s["dummy"]
    sent = {}

    def push(src, dst, sem, off):
        pltpu.make_async_remote_copy(
            src_ref=src, dst_ref=dst, send_sem=send.at[sem], recv_sem=recv.at[sem],
            device_id=device(off), device_id_type=MESH,
        ).start()
        size = 1
        for d in src.shape:
            size *= d
        sent[sem] = sent.get(sem, 0) + size // 1024

    def wait(sems, sem):
        view = dummy.at[pl.ds(0, sent[sem])]
        pltpu.make_async_copy(view, view, sems.at[sem]).wait()

    fk0, fk1, fk2, fk3 = s["fk0"], s["fk1"], s["fk2"], s["fk3"]

    def level(no, fk, h, closed):
        refs = [fk.at[0], fk.at[1]] + [s[f"{n}{no}"] for n in ("wx", "wy", "wz", "ir", "ib", "d", "ur", "ub")]
        return Level(refs, h, 0.25**no, closed)

    l0, l1 = level(0, fk0, 5, False), level(1, fk1, 6, False)
    l2, l3 = level(2, fk2, 8, False), level(3, fk3, 4, True)

    own0 = [fk0.at[a, pl.ds(5, 16), pl.ds(8, 32), pl.ds(0, 128)] for a in range(2)]
    loads = [pltpu.make_async_copy(r, own0[a], s["load"].at[a]) for a, r in enumerate((f_hbm, k_hbm))]
    for c in loads:
        c.start()
    near = [(a, b, c) for a in (-1, 0, 1) for b in (-1, 0, 1) for c in (-1, 0, 1) if (a, b, c) != (0, 0, 0)]
    wide = [(a, b, c) for a in (-2, -1, 0, 1, 2) for b in (-1, 0, 1) for c in (-1, 0, 1) if (a, b, c) != (0, 0, 0)]
    lines = []
    for a in range(3):
        for d in range(1, N):
            lines.append(tuple((d if d <= 4 else d - N) if b == a else 0 for b in range(3)))
    partners = wide + [o for o in lines if o not in wide]
    barrier = pltpu.get_barrier_semaphore()
    for off in partners:
        pl.semaphore_signal(barrier, inc=1, device_id=device(off), device_id_type=MESH)
    for c in loads:
        c.wait()
    pl.semaphore_wait(barrier, len(partners))

    def pack(own, zp, planes, length):
        left = right = None
        for p in range(planes):
            v = own(p)
            group = iota(v.shape, 1) // 8 == p
            a, b = rotate(v, 8 * p, 1), rotate(v, 8 * p - (length - 8), 1)
            left = a if p == 0 else jnp.where(group, a, left)
            right = b if p == 0 else jnp.where(group, b, right)
        zp[0], zp[1] = left, right

    def slabs(src, dst, h, nx, ny, lead, sem):
        for sx in (-1, 0, 1):
            xs = {1: (h + nx - h, h, 0), -1: (h, h, h + nx), 0: (h, nx, h)}[sx]
            for sy in (-1, 0, 1):
                if (sx, sy) == (0, 0):
                    continue
                ys = {1: (8 + ny - 8, 8, 0), -1: (8, 8, 8 + ny), 0: (8, ny, 8)}[sy]
                a = lead + (pl.ds(xs[0], xs[1]), pl.ds(ys[0], ys[1]), pl.ds(0, 128))
                b = lead + (pl.ds(xs[2], xs[1]), pl.ds(ys[2], ys[1]), pl.ds(0, 128))
                push(src.at[a], dst.at[b], sem, (sx, sy, 0))

    def edges(zp, zr, ny, lead, sem):
        for sz in (-1, 1):
            side = 1 if sz == 1 else 0
            for sx in (-1, 0, 1):
                for sy in (-1, 0, 1):
                    ys = {1: (ny - 8, 8, 0), -1: (0, 8, 8 + ny), 0: (0, ny, 8)}[sy]
                    a = (side,) + lead + (pl.ds(ys[0], ys[1]),)
                    b = (1 - side, 1 - sx) + lead + (pl.ds(ys[2], ys[1]),)
                    push(zp.at[a], zr.at[b], sem, (sx, sy, sz))

    def ghost(zr, lead, p, h, nx, base):
        slot, q = (0, nx - h + p) if p < h else (1, p - h) if p < h + nx else (2, p - h - nx)
        right = rotate(zr[(1, slot) + lead], base - 8 * q, 1)
        left = rotate(zr[(0, slot) + lead], 120 - 8 * q, 1)
        lane = iota(right.shape, 1)
        return jnp.where((lane >= base) & (lane < base + 8), right, jnp.where(lane >= 120, left, 0.0))

    def flag(condition):
        return jnp.where(condition, 1.0, 0.0)

    def inside_yz(rows, ny, own_lanes, right_end, lanes):
        row, lane = iota((rows, lanes), 0), iota((rows, lanes), 1)
        in_y = ((row >= 8) | (iy > 0)) & ((row < 8 + ny) | (iy < N - 1))
        in_z = (lane < own_lanes) | ((lane < right_end) & (iz < N - 1)) | ((lane >= right_end) & (iz > 0))
        return jnp.where(in_y & in_z, 1.0, 0.0)

    def inside_x(p, h, nx):
        return flag(ix > 0) if p < h else flag(ix < N - 1) if p >= h + nx else 1.0

    for a in range(2):
        pack(lambda p, a=a: fk0[a, 5 + p, 8:40, 0:128], s["zp0"].at[:, a], 16, 128)
    slabs(fk0, fk0, 5, 16, 32, (slice(None),), 0)
    edges(s["zp0"], s["zr0"], 32, (slice(None),), 1)

    lane_r, lane_c = iota((128, 128), 0), iota((128, 128), 1)
    halve1 = jnp.where((lane_r // 2 == lane_c), 0.125, 0.0)
    halve2 = jnp.where((lane_r // 2 == lane_c) & (lane_c < 32), 0.125, 0.0)

    pair0, pair1, pair2, pair3 = s["pair0"], s["pair1"], s["pair2"], s["pair3"]

    def coarse1():
        flat = pair0.reshape(256, 128)
        return dot(row_pairs(flat, 128), halve1).reshape(8, 16, 128)

    def coarse2():
        flat = pair1.reshape(64, 128)
        return dot(row_pairs(flat, 32), halve2).reshape(4, 8, 128)

    def packed2(value):
        total = value[0]
        for q in range(1, 4):
            total = total + rotate(value[q], 32 * q, 1)
        return total

    row8, col8 = iota((8, 8), 0), iota((8, 8), 1)

    def coarse3():
        place_rows = jnp.where(row8 == 4 * lax.rem(iy, 2) + col8 // 2, 1.0, 0.0)
        total = None
        for dx in range(2):
            group = lax.rem(2 * ix + dx, 8)
            place = jnp.where((lane_r < 32) & (lane_c == 16 * group + lane_r // 2), 0.125, 0.0)
            part = dot(dot(place_rows, pair2[dx]), place)
            total = part if total is None else total + part
        return total

    def gather(tile, g1, g2, g3, sem):
        g1[ix] = tile
        for d in range(1, N):
            push(g1.at[ix], g1.at[ix], sem, (d, 0, 0))
        yield
        wait(recv, sem)
        g2[iy, 0] = g1[0] + g1[1] + g1[2] + g1[3]
        g2[iy, 1] = g1[4] + g1[5] + g1[6] + g1[7]
        for d in range(1, N):
            push(g2.at[iy], g2.at[iy], sem + 1, (0, d, 0))
        yield
        wait(recv, sem + 1)
        for o in range(4):
            for h in range(2):
                g3[iz, h, o] = g2[2 * o, h] + g2[2 * o + 1, h]
        for d in range(1, N):
            push(g3.at[iz], g3.at[iz], sem + 2, (0, 0, d))
        yield
        wait(recv, sem + 2)

    def unpack3(g3, out):
        group = iota((32, 128), 1) // 16
        for h in range(2):
            blocks = [g3[j, h].reshape(32, 128) for j in range(8)]
            for g in range(8):
                total = rotate(blocks[0], 16 * (0 - g), 1)
                for j in range(1, 8):
                    total = jnp.where(group == j, rotate(blocks[j], 16 * (j - g), 1), total)
                out[4 + 8 * h + g] = total

    for i in range(8):
        pair0[i] = fk0[1, 5 + 2 * i, 8:40, 0:128] + fk0[1, 6 + 2 * i, 8:40, 0:128]
    k1_own = coarse1()
    fk1[1, 6:14, 8:24, :] = k1_own
    for i in range(4):
        pair1[i] = k1_own[2 * i] + k1_own[2 * i + 1]
    k2_own = coarse2()
    s["r2"][2, 1, 1, 1] = packed2(k2_own)
    for i in range(2):
        pair2[i] = k2_own[2 * i] + k2_own[2 * i + 1]
    k_gather = gather(coarse3(), s["gk1"], s["gk2"], s["gk3"], 10)
    next(k_gather)

    for lev in (l0, l1, l2):
        for ref in (lev.ur, lev.ub):
            for p in (0, lev.planes - 1):
                ref[p] = jnp.zeros((lev.rows, lev.lanes), F32)
    for p in (0, 1, 2, 3, 20, 21, 22, 23):
        for ref in (l3.ur, l3.ub, fk3.at[0], fk3.at[1]):
            ref[p] = jnp.zeros((32, 128), F32)

    wait(recv, 0)
    wait(recv, 1)
    wait(send, 0)
    myz0 = inside_yz(48, 32, 128, 192, 256)
    for p in range(26):
        for a in range(2):
            g = ghost(s["zr0"], (a,), p, 5, 16, 0)
            if a == 1:
                sx = inside_x(p, 5, 16)
                fk0[1, p, :, 0:128] = fk0[1, p, :, 0:128] * (myz0[:, 0:128] * sx)
                g = g * (myz0[:, 128:256] * sx)
            fk0[a, p, :, 128:256] = g
    l0.prepare(1, 25)
    next(k_gather)
    l0.first(1, 25)
    zero0 = jnp.zeros((48, 256), F32)
    l0.black(2, 24, l0.ub)
    l0.ub[1] = zero0
    l0.ub[24] = zero0
    l0.red(3, 23, l0.ub)
    l0.black(4, 22, l0.ub)
    next(k_gather)
    l0.residual_pairs(5, 8, (8, 40), pair0)
    f1_own = coarse1()
    fk1[0, 6:14, 8:24, :] = f1_own

    for a in range(2):
        pack(lambda p, a=a: fk1[a, 6 + p, 8:24, :], s["zp1"].at[:, a], 8, 64)
    slabs(fk1, fk1, 6, 8, 16, (slice(None),), 2)
    edges(s["zp1"], s["zr1"], 16, (slice(None),), 3)
    pack(lambda p: l0.ub[5 + p, 8:40, 0:128], s["zpu0"], 16, 128)
    slabs(l0.ub, s["v0"], 5, 16, 32, (), 4)
    edges(s["zpu0"], s["zru0"], 32, (), 5)
    s["v0"][5:21, 8:40, 0:128] = l0.ub[5:21, 8:40, 0:128]

    wait(recv, 2)
    wait(recv, 3)
    wait(send, 2)
    myz1 = inside_yz(32, 16, 64, 96, 128)
    lane32 = iota((32, 128), 1)
    for p in range(20):
        for a in range(2):
            v = jnp.where(lane32 < 64, fk1[a, p], ghost(s["zr1"], (a,), p, 6, 8, 64))
            if a == 1:
                v = v * (myz1 * inside_x(p, 6, 8))
            fk1[a, p] = v
    l1.prepare(1, 19)
    l1.first(2, 18)
    l1.black(3, 17, l1.ub)
    l1.ub[2] = jnp.zeros((32, 128), F32)
    l1.ub[17] = jnp.zeros((32, 128), F32)
    l1.red(4, 16, l1.ub)
    l1.black(5, 15, l1.ub)
    l1.residual_pairs(6, 4, (8, 24), pair1)
    s["r2"][2, 1, 1, 0] = packed2(coarse2())

    r2 = s["r2"]
    for off in wide:
        push(r2.at[2, 1, 1], r2.at[2 - off[0], 1 - off[1], 1 - off[2]], 6, off)
    pack(lambda p: l1.ub[6 + p, 8:24, :], s["zpu1"], 8, 64)
    slabs(l1.ub, s["v1"], 6, 8, 16, (), 7)
    edges(s["zpu1"], s["zru1"], 16, (), 8)
    s["v1"][6:14, 8:24, :] = l1.ub[6:14, 8:24, :]

    for _ in k_gather:
        pass
    unpack3(s["gk3"], fk3.at[1])
    l3.prepare(4, 20)

    wait(recv, 6)
    lane8 = iota((8, 128), 1)

    def unpack2(block, p, by):
        b, q = divmod(p, 4)
        own = rotate(block(b, by, 1), -32 * q, 1)
        right = rotate(block(b, by, 2), 32 * (1 - q), 1)
        left = rotate(block(b, by, 0), 32 * (3 - q), 1)
        v = jnp.where(lane8 < 32, own, jnp.where(lane8 < 64, right, jnp.where(lane8 >= 96, left, 0.0)))
        return v

    row24, lane24 = iota((24, 128), 0), iota((24, 128), 1)
    in_y = ((row24 >= 8) | (iy > 0)) & ((row24 < 16) | (iy < N - 1))
    in_z = (lane24 < 32) | ((lane24 < 64) & (iz < N - 1)) | ((lane24 >= 96) & (iz > 0))
    myz2 = jnp.where(in_y & in_z, 1.0, 0.0)
    for p in range(20):
        b = p // 4
        sx = [flag(ix > 1), flag(ix > 0), 1.0, flag(ix < N - 1), flag(ix < N - 2)][b]
        for a in range(2):
            for by in range(3):
                v = unpack2(lambda i, j, k, a=a: r2[i, j, k, a], p, by)
                if a == 1:
                    v = v * (myz2[8 * by : 8 * by + 8] * sx)
                fk2[a, p, 8 * by : 8 * by + 8, :] = v
    l2.prepare(1, 19)
    l2.first(4, 16)
    l2.black(5, 15, l2.ub)
    l2.ub[4] = jnp.zeros((24, 128), F32)
    l2.ub[15] = jnp.zeros((24, 128), F32)
    l2.red(6, 14, l2.ub)
    l2.black(7, 13, l2.ub)
    l2.residual_pairs(8, 2, (8, 16), pair2)
    f_gather = gather(coarse3(), s["gf1"], s["gf2"], s["gf3"], 13)
    next(f_gather)
    ru2 = s["ru2"]
    total = l2.ub[8, 8:16, :]
    total = jnp.where(lane8 < 32, total, 0.0)
    for q in range(1, 4):
        total = total + rotate(jnp.where(lane8 < 32, l2.ub[8 + q, 8:16, :], 0.0), 32 * q, 1)
    ru2[2, 1, 1] = total
    for off in wide:
        push(ru2.at[2, 1, 1], ru2.at[2 - off[0], 1 - off[1], 1 - off[2]], 9, off)
    pair3_flat = pair3.reshape(8 * 32, 128)

    def coarse4():
        rows = row_pairs(pair3_flat, 128).reshape(8, 16, 128)
        out = None
        for h in range(2):
            place = jnp.where(lane_c == 64 * h + lane_r // 2, 0.125, 0.0)
            part = dot(rows[4 * h : 4 * h + 4].reshape(64, 128), place)
            out = part if out is None else out + part
        return out.reshape(4, 16, 128)

    for i in range(8):
        pair3[i] = fk3[1, 4 + 2 * i] + fk3[1, 5 + 2 * i]
    k4 = coarse4()
    shape4 = (4, 16, 128)
    row4, lane4 = iota(shape4, 1), iota(shape4, 2)
    z4 = lane4 & 63

    def cat(parts):
        return jnp.concatenate(parts, axis=0)

    def x_below(v):
        return cat([rotate(v[3], 64, 1)[None], v[0:3]])

    def x_above(v):
        return cat([v[1:4], rotate(v[0], 64, 1)[None]])

    def roll3(v, shift, axis):
        flat = [rotate(v[i], shift, axis)[None] for i in range(4)]
        return cat(flat)

    plane4 = iota(shape4, 0)
    first_x = (plane4 == 0) & (lane4 < 64)
    last_x = (plane4 == 3) & (lane4 >= 64)
    hs4 = 0.5 * 0.25**4
    kxl, kxu = jnp.where(first_x, 0.0, x_below(k4)), jnp.where(last_x, 0.0, x_above(k4))
    kyl = jnp.where(row4 == 0, 0.0, roll3(k4, 1, 0))
    kyu = jnp.where(row4 == 15, 0.0, roll3(k4, -1, 0))
    kzl = jnp.where(z4 == 0, 0.0, roll3(k4, 1, 1))
    kzu = jnp.where(z4 == 63, 0.0, roll3(k4, -1, 1))
    w4 = s["w4"]
    inv4 = 1.0 / (hs4 * (6.0 * k4 + kxl + kxu + kyl + kyu + kzl + kzu))
    odd4 = (plane4 + row4 + lane4) & 1
    w4[0] = jnp.where(first_x, 0.0, hs4 * (k4 + kxl))
    w4[1] = jnp.where(last_x, 0.0, hs4 * (k4 + kxu))
    w4[2] = jnp.where(row4 == 0, 0.0, hs4 * (k4 + kyl))
    w4[3] = jnp.where(row4 == 15, 0.0, hs4 * (k4 + kyu))
    w4[4] = jnp.where(z4 == 0, 0.0, hs4 * (k4 + kzl))
    w4[5] = jnp.where(z4 == 63, 0.0, hs4 * (k4 + kzu))
    w4[6] = jnp.where(odd4 == 0, inv4, 0.0)
    w4[7] = jnp.where(odd4 == 1, inv4, 0.0)

    for _ in f_gather:
        pass
    unpack3(s["gf3"], fk3.at[0])
    l3.first(4, 20)
    l3.black(4, 20, l3.ub)
    l3.red(4, 20, l3.ub)
    l3.black(4, 20, l3.ub)
    l3.residual_pairs(4, 8, (0, 32), pair3)
    f4 = coarse4()
    w4[8] = f4

    def around4(v):
        total = w4[0] * x_below(v) + w4[1] * x_above(v)
        total = total + (w4[2] * roll3(v, 1, 0) + w4[3] * roll3(v, -1, 0))
        return total + (w4[4] * roll3(v, 1, 1) + w4[5] * roll3(v, -1, 1))

    def bottom(i, carry):
        black = carry[1]
        red = w4[6] * (w4[8] + around4(black))
        black = w4[7] * (w4[8] + around4(red))
        return (red, black)

    zero4 = jnp.zeros(shape4, F32)
    red4, black4 = lax.fori_loop(0, BOTTOM, bottom, (zero4, zero4))
    u4 = red4 + black4

    for h in range(2):
        place = jnp.where(lane_r == 64 * h + lane_c // 2, 1.0, 0.0)
        wide4 = dot(u4.reshape(64, 128), place)
        flat = pair3_flat
        flat[pl.ds(128 * h, 64, 2), :] = wide4
        flat[pl.ds(128 * h + 1, 64, 2), :] = wide4

    def add(lev, black, p, corr):
        black[p] = jnp.where(lev.ib[p] > 0.0, black[p] + corr, 0.0)

    for i in range(8):
        corr = pair3[i]
        add(l3, l3.ub, 4 + 2 * i, corr)
        add(l3, l3.ub, 5 + 2 * i, corr)
    for _ in range(2):
        l3.red(4, 20, l3.ub)
        l3.black(4, 20, l3.ub)

    wait(recv, 9)
    v2 = s["v2"]
    for p in range(20):
        for by in range(3):
            v2[p, 8 * by : 8 * by + 8, :] = unpack2(lambda i, j, k: ru2[i, j, k], p, by)
    zoff = jnp.where(lane_c < 64, lane_c, lane_c - 128)
    source_lane = 16 * iz + ((zoff + 128) // 2 - 64)
    spread_z = jnp.where((lane_r == source_lane) & ((lane_c < 64) | (lane_c >= 96)), 1.0, 0.0)
    spread_y = jnp.where(iota((24, 32), 1) == 4 * iy - 4 + iota((24, 32), 0) // 2, 1.0, 0.0)
    for j in range(10):
        p3 = 2 * ix + j
        u3 = l3.ur[p3] + l3.ub[p3]
        corr = dot(spread_y, dot(u3, spread_z))
        add(l2, v2, 2 * j, corr) if j > 0 else None
        add(l2, v2, 2 * j + 1, corr)
    l2.red(2, 18, v2)
    l2.black(3, 17, v2)
    l2.red(4, 16, v2)
    l2.black(5, 15, v2)

    wait(recv, 7)
    wait(recv, 8)
    v1 = s["v1"]
    for p in range(20):
        v1[p] = jnp.where(lane32 < 64, v1[p], ghost(s["zru1"], (), p, 6, 8, 64))
    spread1 = jnp.where(lane_r == jnp.where(lane_c >= 96, 64 + lane_c // 2, lane_c // 2), 1.0, 0.0)
    up1 = s["up1"]
    coarse = (l2.ur[5:15] + v2[5:15]).reshape(240, 128)
    up1[...] = dot(coarse, spread1).reshape(10, 24, 128)
    tall1 = s["tall1"]
    for j in range(10):
        part = up1[j, 4:20, :]
        tall1[pl.ds(0, 16, 2), :] = part
        tall1[pl.ds(1, 16, 2), :] = part
        corr = tall1[...]
        for p in (2 * j, 2 * j + 1):
            if 0 < p < 19:
                add(l1, v1, p, corr)
    l1.red(1, 19, v1)
    l1.black(2, 18, v1)
    l1.red(3, 17, v1)
    l1.black(4, 16, v1)

    wait(recv, 4)
    wait(recv, 5)
    v0 = s["v0"]
    for p in range(1, 25):
        v0[p, :, 128:256] = ghost(s["zru0"], (), p, 5, 16, 0)
    spread0 = jnp.where(iota((128, 256), 0) == iota((128, 256), 1) // 2, 1.0, 0.0)
    up0 = s["up0"]
    coarse = (l1.ur[4:16] + v1[4:16]).reshape(384, 128)
    up0[...] = dot(coarse, spread0).reshape(12, 32, 256)
    tall0 = s["tall0"]
    for j in range(12):
        for t in range(2):
            part = up0[j, 4:28, 128 * t : 128 * t + 128]
            tall0[t, pl.ds(0, 24, 2), :] = part
            tall0[t, pl.ds(1, 24, 2), :] = part
        for t in range(2):
            corr = tall0[t]
            for p in (1 + 2 * j, 2 + 2 * j):
                lanes = slice(128 * t, 128 * t + 128)
                v0[p, :, lanes] = jnp.where(l0.ib[p, :, lanes] > 0.0, v0[p, :, lanes] + corr, 0.0)
    l0.red(2, 24, v0)
    l0.black(3, 23, v0)
    l0.red(4, 22, v0)
    l0.black(5, 21, v0)
    out_ref[...] = l0.ur[5:21, 8:40, 0:128] + v0[5:21, 8:40, 0:128]
    for sem in sorted(sent):
        if sem not in (0, 2):
            wait(send, sem)


def vmem(*shape):
    return pltpu.VMEM(shape, F32)


def scratch_shapes():
    shapes = {}
    for no, shape in enumerate([(26, 48, 256), (20, 32, 128), (20, 24, 128), (24, 32, 128)]):
        shapes[f"fk{no}"] = vmem(2, *shape)
        for name in ("wx", "wy", "wz", "ir", "ib", "d", "ur", "ub"):
            shapes[f"{name}{no}"] = vmem(*shape)
        if no < 3:
            shapes[f"v{no}"] = vmem(*shape)
    shapes["zp0"], shapes["zr0"] = vmem(2, 2, 32, 128), vmem(2, 3, 2, 48, 128)
    shapes["zpu0"], shapes["zru0"] = vmem(2, 32, 128), vmem(2, 3, 48, 128)
    shapes["zp1"], shapes["zr1"] = vmem(2, 2, 16, 128), vmem(2, 3, 2, 32, 128)
    shapes["zpu1"], shapes["zru1"] = vmem(2, 16, 128), vmem(2, 3, 32, 128)
    shapes["r2"], shapes["ru2"] = vmem(5, 3, 3, 2, 8, 128), vmem(5, 3, 3, 8, 128)
    for name in "kf":
        shapes[f"g{name}1"] = vmem(8, 8, 128)
        shapes[f"g{name}2"] = vmem(8, 2, 8, 128)
        shapes[f"g{name}3"] = vmem(8, 2, 4, 8, 128)
    shapes["pair0"], shapes["pair1"] = vmem(8, 32, 128), vmem(4, 16, 128)
    shapes["pair2"], shapes["pair3"] = vmem(2, 8, 128), vmem(8, 32, 128)
    shapes["w4"] = vmem(9, 4, 16, 128)
    shapes["up0"], shapes["tall0"] = vmem(12, 32, 256), vmem(2, 48, 128)
    shapes["up1"], shapes["tall1"] = vmem(10, 24, 128), vmem(32, 128)
    shapes["dummy"] = vmem(256, 8, 128)
    shapes["send"] = pltpu.SemaphoreType.DMA((16,))
    shapes["recv"] = pltpu.SemaphoreType.DMA((16,))
    shapes["load"] = pltpu.SemaphoreType.DMA((2,))
    return shapes


SCRATCH = scratch_shapes()


def on_device(source_term, conductivity):
    return pl.pallas_call(
        kernel,
        out_shape=jax.ShapeDtypeStruct((16, 32, 128), F32),
        in_specs=[pl.BlockSpec(memory_space=pl.ANY)] * 2,
        out_specs=pl.BlockSpec(memory_space=pltpu.VMEM),
        scratch_shapes=list(SCRATCH.values()),
        compiler_params=pltpu.CompilerParams(
            collective_id=0, has_side_effects=True, vmem_limit_bytes=48 * 2**20
        ),
        name="vcycle",
    )(source_term, conductivity)


def solution(mesh):
    spec = P("gx", "gy", "gz")
    return jax.shard_map(
        on_device, mesh=mesh, in_specs=(spec, spec), out_specs=spec, check_vma=False
    )
```

time: 1320 us -> 103 us (0.08); the launches traced: 1300 us -> 103 us
  starting transfers between devices: 525 us -> 0 us
  local copies, waits for them, and re-layouts: 257 us -> 2.6 us
  other arithmetic: 247 us -> 0 us
  waiting for transfers between devices: 155 us -> 0 us
  blocking collectives: 110 us -> 0 us
  Pallas kernels: 0 us -> 101 us
    ppermute x180 -> x0, starting transfers between devices: 525 us -> none  [the longest x90 373 us: extended(): before = lax.ppermute(last, axis, up)]
    ppermute x180 -> x0, waiting for transfers between devices: 155 us -> none  [the longest x90 151 us: extended(): after = lax.ppermute(initial, axis, down)]
    select_n x64 -> x0, other arithmetic: 121 us -> none  [relaxation(): iterate = jnp.where(colour_mask, updated, iterate)]
    all_gather x6 -> x0, blocking collectives: 110 us -> none  [the longest x2 42.7 us: join_x(): return lax.all_gather(values, 'gx', axis=0, tiled=True)]
    unnamed x269 -> x5, local copies, waits for them, and re-layouts: 112 us -> 2.6 us
    pallas_call x0 -> x1, Pallas kernels: none -> 101 us  [on_device(): pl.pallas_call(kernel, out_shape=jax.ShapeDtypeStruct((16, 32, 128), F32)...]
    reshape x13 -> x0, local copies, waits for them, and re-layouts: 64.4 us -> none  [the longest x7 55.3 us: coarsen(): blocks = values.reshape(size_x // 2, 2, size_y // 2, 2, size_z // 2, 2)]
    concatenate x62 -> x0, other arithmetic: 50.8 us -> none  [extended(): value = jnp.concatenate([before, value, after], axis=dim)]
  transfers between devices with their start and end apart: 180 -> 0, of which waited for: 56 -> 0; matrix products, arithmetic and copies ran while one was open for 21% -> 0% of each run, Pallas kernels for 0% -> 0%
where the time goes in v1:
time: 103 us
  Pallas kernels  101 us (98%)
  local copies, waits for them, and re-layouts  2.6 us (3%)
    pallas_call x1, Pallas kernels, on_device(): pl.pallas_call(kernel, out_shape=jax.ShapeDtypeStruct((16, 32, 128), F32)...  101 us
    unnamed x5, local copies, waits for them, and re-layouts  2.6 us

profile of v1, /device:TPU:1, one launch (start us, length us, event | category | flops | bytes accessed | tf_op | source)
XLA Modules:
  0.0 103.2 jit_solution(16422497407293968783)
XLA Ops:
  0.0 0.0 copy-start
  0.0 0.9 copy-done
  1.0 0.0 copy-start.1
  1.0 0.9 copy-done.1
  1.9 100.6 %vcycle.1 = f32[16,32,128]{2,1,0:T(8,128)S(1)} custom-call(f32[16,32,128]{2,1,0:T(8,128)S(1)} %copy-done, f32[16,32,128]{2,1,0:T(8,128)S(1)} %copy-done.1), custom_call_target="tpu_custom_call" | custom-call | tf_op jit(solution)/shard_map/vcycle/pallas_call | solution.py:624
  102.5 0.7 copy.4
Async XLA Ops:
  0.0 0.9 copy-start
  1.0 0.9 copy-start.1

commit v2 on v1

v2 whole, which is shorter than its diff:
```python
import functools

import jax
import jax.numpy as jnp
from jax import lax
from jax.experimental import pallas as pl
from jax.experimental.pallas import tpu as pltpu
from jax.sharding import PartitionSpec as P

MESH = pl.DeviceIdType.MESH
AXES = ("gx", "gy", "gz")
N = 8
BOTTOM = 16
F32 = jnp.float32


def iota(shape, axis):
    return lax.broadcasted_iota(jnp.int32, shape, axis)


def halves(a):
    high = a.astype(jnp.bfloat16)
    return high, (a - high.astype(F32)).astype(jnp.bfloat16)


def product(a, b):
    return lax.dot_general(a, b, (((1,), (0,)), ((), ())), preferred_element_type=F32)


def spread(a, b):
    high, low = halves(a)
    b = b.astype(jnp.bfloat16)
    return product(high, b) + product(low, b)


def select_rows(a, b):
    high, low = halves(b)
    a = a.astype(jnp.bfloat16)
    return product(a, high) + product(a, low)


def rotate(a, shift, axis):
    shift = shift % a.shape[axis]
    return a if shift == 0 else pltpu.roll(a, shift, axis)


class Level:
    def __init__(self, s, no, fk, scale, closed, block):
        self.f, self.k = fk.at[0], fk.at[1]
        self.xin, self.dr, self.db = s[f"xin{no}"], s[f"dr{no}"], s[f"db{no}"]
        self.v = {"r": s[f"vr{no}"], "b": s[f"vb{no}"]}
        self.xo, self.y, self.z, self.i, self.g = (
            {c: s[f"{n}{c}{no}"] for c in "rb"} for n in ("xo", "wy", "wz", "inv", "src")
        )
        self.pairs, self.rows, self.lanes = self.xin.shape
        self.scale, self.closed, self.block = (scale, closed, block)

    def even(self):
        shape = (self.rows, self.lanes)
        return (iota(shape, 0) + iota(shape, 1)) & 1 == 0

    def loop(self, lo, hi, body):
        block = min(self.block, hi - lo)
        if block == hi - lo:
            for j in range(lo, hi):
                body(j)
            return

        def step(i, carry):
            for t in range(block):
                body(lo + i * block + t)
            return carry

        lax.fori_loop(0, (hi - lo) // block, step, 0)
        for j in range(lo + (hi - lo) // block * block, hi):
            body(j)

    def prepare(self, lo, hi, sources=True):
        shape = (self.rows, self.lanes)
        hs = 0.5 * self.scale

        def one(p):
            k = self.k[p]
            kyl, kyu = rotate(k, 1, 0), rotate(k, -1, 0)
            kzl, kzu = rotate(k, 1, 1), rotate(k, -1, 1)
            wy, wz = hs * (k + kyl), hs * (k + kzl)
            if self.closed:
                row, lane = iota(shape, 0), iota(shape, 1)
                kyl = jnp.where(row == 0, 0.0, kyl)
                kyu = jnp.where(row == self.rows - 1, 0.0, kyu)
                kzl = jnp.where(lane == 0, 0.0, kzl)
                kzu = jnp.where(lane == self.lanes - 1, 0.0, kzu)
                wy = jnp.where(row == 0, 0.0, wy)
                wz = jnp.where(lane == 0, 0.0, wz)
            diag = hs * (6.0 * k + self.k[p - 1] + self.k[p + 1] + kyl + kyu + kzl + kzu)
            inside = k > 0.0
            inv = jnp.where(inside, 1.0 / jnp.where(inside, diag, 1.0), 0.0)
            return wy, wz, inv, diag

        def body(j):
            even = self.even()
            p = 2 * j - 1
            first, second = one(p), one(p + 1)
            below = hs * (self.k[p] + self.k[p - 1])
            above = hs * (self.k[p + 2] + self.k[p + 1])
            self.xin[j] = hs * (self.k[p] + self.k[p + 1])
            self.xo["r"][j] = jnp.where(even, below, above)
            self.xo["b"][j] = jnp.where(even, above, below)
            for ref, n in ((self.y, 0), (self.z, 1), (self.i, 2)):
                ref["r"][j] = jnp.where(even, first[n], second[n])
                ref["b"][j] = jnp.where(even, second[n], first[n])
            self.dr[j] = jnp.where(even, first[3], second[3])
            self.db[j] = jnp.where(even, second[3], first[3])

        self.loop(lo, hi, body)

    def sources(self, lo, hi):
        def body(j):
            even = self.even()
            a, b = self.f[2 * j - 1], self.f[2 * j]
            red = jnp.where(even, a, b)
            self.g["r"][j] = red
            self.g["b"][j] = jnp.where(even, b, a)
            self.v["r"][j] = self.i["r"][j] * red

        self.loop(lo, hi, body)

    def around(self, colour, other, j):
        far = "b" if colour == "r" else "r"
        u, before, after = other[j], other[j - 1], other[j + 1]
        if colour == "b":
            before, after = after, before
        total = self.xin[j] * u + self.xo[colour][j] * jnp.where(self.even(), before, after)
        total = total + (self.y[colour][j] * rotate(u, 1, 0) + rotate(self.y[far][j] * u, -1, 0))
        return total + (self.z[colour][j] * rotate(u, 1, 1) + rotate(self.z[far][j] * u, -1, 1))

    def half(self, colour, black, lo, hi):
        target, other = (self.v["r"], black) if colour == "r" else (black, self.v["r"])

        def body(j):
            target[j] = self.i[colour][j] * (self.g[colour][j] + self.around(colour, other, j))

        self.loop(lo, hi, body)

    def sweep(self, black, red_range, black_range):
        self.half("r", black, *red_range)
        self.half("b", black, *black_range)

    def residual(self, lo, hi, rows, out):
        def body(j):
            r, b = self.v["r"], self.v["b"]
            red = self.g["r"][j] - (self.dr[j] * r[j] - self.around("r", b, j))
            black = self.g["b"][j] - (self.db[j] * b[j] - self.around("b", r, j))
            out[j - lo] = (red + black)[rows[0] : rows[1], 0:128]

        self.loop(lo, hi, body)

    def correct(self, black, j, value):
        black[j] = jnp.where(self.i["b"][j] > 0.0, black[j] + value, 0.0)

    def planes(self, black, j):
        r, b, even = self.v["r"][j], black[j], self.even()
        return jnp.where(even, r, b), jnp.where(even, b, r)


def row_pairs(ref, count):
    return ref[pl.ds(0, count, 2), :] + ref[pl.ds(1, count, 2), :]


def kernel(f_hbm, k_hbm, out_ref, *scratch):
    names = list(SCRATCH)
    s = dict(zip(names, scratch))
    ix, iy, iz = (lax.axis_index(a) for a in AXES)
    me = (ix, iy, iz)

    def device(off):
        return tuple(lax.rem(me[a] + (off[a] + N), N) for a in range(3))

    send, recv, dummy = s["send"], s["recv"], s["dummy"]
    sent = {}

    def push(src, dst, sem, off):
        pltpu.make_async_remote_copy(
            src_ref=src, dst_ref=dst, send_sem=send.at[sem], recv_sem=recv.at[sem],
            device_id=device(off), device_id_type=MESH,
        ).start()
        size = 1
        for d in src.shape:
            size *= d
        sent[sem] = sent.get(sem, 0) + size // 1024

    def wait(sems, sem):
        view = dummy.at[pl.ds(0, sent[sem])]
        pltpu.make_async_copy(view, view, sems.at[sem]).wait()

    fk0, fk1, fk2, fk3 = s["fk0"], s["fk1"], s["fk2"], s["fk3"]

    l0, l1 = Level(s, 0, fk0, 1.0, False, 2), Level(s, 1, fk1, 0.25, False, 12)
    l2, l3 = Level(s, 2, fk2, 0.25**2, False, 12), Level(s, 3, fk3, 0.25**3, True, 12)

    own0 = [fk0.at[a, pl.ds(5, 16), pl.ds(8, 32), pl.ds(0, 128)] for a in range(2)]
    loads = [pltpu.make_async_copy(r, own0[a], s["load"].at[a]) for a, r in enumerate((f_hbm, k_hbm))]
    for c in loads:
        c.start()
    near = [(a, b, c) for a in (-1, 0, 1) for b in (-1, 0, 1) for c in (-1, 0, 1) if (a, b, c) != (0, 0, 0)]
    wide = [(a, b, c) for a in (-2, -1, 0, 1, 2) for b in (-1, 0, 1) for c in (-1, 0, 1) if (a, b, c) != (0, 0, 0)]
    lines = []
    for a in range(3):
        for d in range(1, N):
            lines.append(tuple((d if d <= 4 else d - N) if b == a else 0 for b in range(3)))
    partners = wide + [o for o in lines if o not in wide]
    barrier = pltpu.get_barrier_semaphore()
    for off in partners:
        pl.semaphore_signal(barrier, inc=1, device_id=device(off), device_id_type=MESH)
    for c in loads:
        c.wait()
    pl.semaphore_wait(barrier, len(partners))

    def pack(own, zp, planes, length):
        left = right = None
        for p in range(planes):
            v = own(p)
            group = iota(v.shape, 1) // 8 == p
            a, b = rotate(v, 8 * p, 1), rotate(v, 8 * p - (length - 8), 1)
            left = a if p == 0 else jnp.where(group, a, left)
            right = b if p == 0 else jnp.where(group, b, right)
        zp[0], zp[1] = left, right

    def slabs(src, dst, start, nx, w, ny, lead, sem, corners=None):
        for sx in (-1, 0, 1):
            for sy in (-1, 0, 1):
                if (sx, sy) == (0, 0):
                    continue
                xs = {1: (start + nx - w, w, start - w), -1: (start, w, start + nx), 0: (start, nx, start)}[sx]
                ys = {1: (8 + ny - 8, 8, 0), -1: (8, 8, 8 + ny), 0: (8, ny, 8)}[sy]
                a = lead + (pl.ds(xs[0], xs[1]), pl.ds(ys[0], ys[1]), pl.ds(0, 128))
                b = lead + (pl.ds(xs[2], xs[1]), pl.ds(ys[2], ys[1]), pl.ds(0, 128))
                push(src.at[a], dst.at[b], sem, (sx, sy, 0))

    def edges(zp, zr, ny, lead, sem, columns=(-1, 0, 1)):
        for sz in (-1, 1):
            side = 1 if sz == 1 else 0
            for sx in columns:
                for sy in (-1, 0, 1):
                    ys = {1: (ny - 8, 8, 0), -1: (0, 8, 8 + ny), 0: (0, ny, 8)}[sy]
                    a = (side,) + lead + (pl.ds(ys[0], ys[1]),)
                    b = (1 - side, 1 - sx) + lead + (pl.ds(ys[2], ys[1]),)
                    push(zp.at[a], zr.at[b], sem, (sx, sy, sz))

    def place(right, left, base):
        lane = iota(right.shape, 1)
        return jnp.where((lane >= base) & (lane < base + 8), right, jnp.where(lane >= 120, left, 0.0))

    def slot(p, start, nx):
        return (0, p - start + nx) if p < start else (1, p - start) if p < start + nx else (2, p - start - nx)

    def ghost(zr, lead, p, start, nx, base):
        b, q = slot(p, start, nx)
        right = rotate(zr[(1, b) + lead], base - 8 * q, 1)
        left = rotate(zr[(0, b) + lead], 120 - 8 * q, 1)
        return place(right, left, base)

    def flag(condition):
        return jnp.where(condition, 1.0, 0.0)

    def inside_yz(rows, ny, own_lanes, right_end, lanes):
        row, lane = iota((rows, lanes), 0), iota((rows, lanes), 1)
        in_y = ((row >= 8) | (iy > 0)) & ((row < 8 + ny) | (iy < N - 1))
        in_z = (lane < own_lanes) | ((lane < right_end) & (iz < N - 1)) | ((lane >= right_end) & (iz > 0))
        return jnp.where(in_y & in_z, 1.0, 0.0)

    def inside_x(p, h, nx):
        return flag(ix > 0) if p < h else flag(ix < N - 1) if p >= h + nx else 1.0

    zp0, ze0, zr0, zs0 = s["zp0"], s["ze0"], s["zr0"], s["zs0"]
    for a in range(2):
        pack(lambda p, a=a: fk0[a, 5 + p, 8:40, 0:128], zp0.at[:, a], 16, 128)
    slabs(fk0, fk0, 5, 16, 4, 32, (slice(None),), 0)
    for sx, a, b in ((1, 16 + 0, 0), (-1, 9, 25)):
        push(fk0.at[1, a, pl.ds(8, 32), pl.ds(0, 128)], fk0.at[1, b, pl.ds(8, 32), pl.ds(0, 128)], 0, (sx, 0, 0))
    edges(zp0, zr0, 32, (slice(None),), 1, (0,))
    lane32 = iota((32, 128), 1)
    for side in range(2):
        fs, ks = zp0[side, 0], zp0[side, 1]
        v = jnp.where(lane32 < 32, fs, rotate(fs, -64, 1))
        ze0[side] = jnp.where(lane32 < 64, v, jnp.where(lane32 < 96, rotate(ks, 64, 1), ks))
    edges(ze0, zs0, 32, (), 1, (-1, 1))

    def ghost0(a, p):
        b, q = slot(p, 5, 16)
        if b == 1:
            return ghost(zr0, (a,), p, 5, 16, 0)
        if not 0 < p < 25:
            return jnp.zeros((48, 128), F32)
        at = 64 * a + (8 * q if b == 2 else 32 + 8 * (q - 12))
        return place(rotate(zs0[1, b], -at, 1), rotate(zs0[0, b], 120 - at, 1), 0)

    lane_r, lane_c = iota((128, 128), 0), iota((128, 128), 1)
    halve1 = jnp.where((lane_r // 2 == lane_c), 0.125, 0.0)
    halve2 = jnp.where((lane_r // 2 == lane_c) & (lane_c < 32), 0.125, 0.0)

    pair0, pair1, pair2, pair3 = s["pair0"], s["pair1"], s["pair2"], s["pair3"]

    def coarse1():
        flat = pair0.reshape(256, 128)
        return spread(row_pairs(flat, 128), halve1).reshape(8, 16, 128)

    def coarse2():
        flat = pair1.reshape(64, 128)
        return spread(row_pairs(flat, 32), halve2).reshape(4, 8, 128)

    def packed2(value):
        total = value[0]
        for q in range(1, 4):
            total = total + rotate(value[q], 32 * q, 1)
        return total

    row8, col8 = iota((8, 8), 0), iota((8, 8), 1)

    def coarse3():
        place_rows = jnp.where(row8 == 4 * lax.rem(iy, 2) + col8 // 2, 1.0, 0.0)
        total = None
        for dx in range(2):
            group = lax.rem(2 * ix + dx, 8)
            into = jnp.where((lane_r < 32) & (lane_c == 16 * group + lane_r // 2), 0.125, 0.0)
            part = spread(select_rows(place_rows, pair2[dx]), into)
            total = part if total is None else total + part
        return total

    def gather(tile, g1, g2, g3, sem):
        g1[ix] = tile
        for d in range(1, N):
            push(g1.at[ix], g1.at[ix], sem, (d, 0, 0))
        yield
        wait(recv, sem)
        g2[iy, 0] = g1[0] + g1[1] + g1[2] + g1[3]
        g2[iy, 1] = g1[4] + g1[5] + g1[6] + g1[7]
        for d in range(1, N):
            push(g2.at[iy], g2.at[iy], sem + 1, (0, d, 0))
        yield
        wait(recv, sem + 1)
        for o in range(4):
            for h in range(2):
                g3[iz, h, o] = g2[2 * o, h] + g2[2 * o + 1, h]
        for d in range(1, N):
            push(g3.at[iz], g3.at[iz], sem + 2, (0, 0, d))
        yield
        wait(recv, sem + 2)

    def unpack3(g3, out):
        group = iota((32, 128), 1) // 16
        for h in range(2):
            blocks = [g3[j, h].reshape(32, 128) for j in range(8)]
            for g in range(8):
                total = rotate(blocks[0], 16 * (0 - g), 1)
                for j in range(1, 8):
                    total = jnp.where(group == j, rotate(blocks[j], 16 * (j - g), 1), total)
                out[1 + 8 * h + g] = total

    for i in range(8):
        pair0[i] = fk0[1, 5 + 2 * i, 8:40, 0:128] + fk0[1, 6 + 2 * i, 8:40, 0:128]
    k1_own = coarse1()
    fk1[1, 7:15, 8:24, :] = k1_own
    for i in range(4):
        pair1[i] = k1_own[2 * i] + k1_own[2 * i + 1]
    k2_own = coarse2()
    rk2 = s["rk2"]
    rk2[2, 1, 1] = packed2(k2_own)
    for i in range(2):
        pair2[i] = k2_own[2 * i] + k2_own[2 * i + 1]
    k_gather = gather(coarse3(), s["gk1"], s["gk2"], s["gk3"], 10)
    pack(lambda p: fk1[1, 7 + p, 8:24, :], s["zk1"], 8, 64)

    for lev, last in ((l0, 13), (l1, 11), (l2, 11), (l3, 9)):
        for colour in "rb":
            for j in (0, last):
                lev.v[colour][j] = jnp.zeros((lev.rows, lev.lanes), F32)
    for j in (0, 13):
        s["v0"][j] = jnp.zeros((48, 256), F32)
    for j in (0, 11):
        s["v1"][j] = jnp.zeros((32, 128), F32)
        s["v2"][j] = jnp.zeros((24, 128), F32)
    for p in (0, 21):
        fk1[1, p] = jnp.zeros((32, 128), F32)
        fk2[1, p] = jnp.zeros((24, 128), F32)
    for p in (1, 20):
        fk1[0, p] = jnp.zeros((32, 128), F32)
    for p in (0, 17):
        fk3[1, p] = jnp.zeros((32, 128), F32)
    u3 = s["u3"]
    for p in (0, 1, 2, 3, 20, 21, 22, 23):
        u3[p] = jnp.zeros((32, 128), F32)

    wait(recv, 0)
    wait(recv, 1)
    wait(send, 0)
    slabs(fk1, fk1, 7, 8, 6, 16, (1,), 2)
    edges(s["zk1"], s["zrk1"], 16, (), 3)
    for off in wide:
        push(rk2.at[2, 1, 1], rk2.at[2 - off[0], 1 - off[1], 1 - off[2]], 16, off)
    next(k_gather)
    myz0 = inside_yz(48, 32, 128, 192, 256)
    row48 = iota((48, 128), 0)
    for p in range(26):
        for a in range(2):
            g = ghost0(a, p)
            if a == 1:
                sx = inside_x(p, 5, 16)
                main = fk0[1, p, :, 0:128] * (myz0[:, 0:128] * sx)
                if not 0 < p < 25:
                    main = jnp.where((row48 >= 8) & (row48 < 40), main, 0.0)
                fk0[1, p, :, 0:128] = main
                g = g * (myz0[:, 128:256] * sx)
            fk0[a, p, :, 128:256] = g
    l0.prepare(1, 13)
    l0.sources(1, 13)
    l0.half("b", l0.v["b"], 1, 13)
    l0.sweep(l0.v["b"], (2, 12), (2, 12))
    l0.residual(3, 11, (8, 40), pair0)
    f1_own = coarse1()
    fk1[0, 7:15, 8:24, :] = f1_own

    pack(lambda p: fk1[0, 7 + p, 8:24, :], s["zf1"], 8, 64)
    slabs(fk1, fk1, 7, 8, 5, 16, (0,), 4)
    edges(s["zf1"], s["zrf1"], 16, (), 5)
    wait(recv, 2)
    wait(recv, 3)
    wait(send, 2)
    myz1 = inside_yz(32, 16, 64, 96, 128)
    for p in range(1, 21):
        v = jnp.where(lane32 < 64, fk1[1, p], ghost(s["zrk1"], (), p, 7, 8, 64))
        fk1[1, p] = v * (myz1 * inside_x(p, 7, 8))
    l1.prepare(1, 11)
    next(k_gather)

    lane8 = iota((8, 128), 1)

    def unpack2(block, b, q, by):
        own = rotate(block(b, by, 1), -32 * q, 1)
        right = rotate(block(b, by, 2), 32 * (1 - q), 1)
        left = rotate(block(b, by, 0), 32 * (3 - q), 1)
        return jnp.where(lane8 < 32, own, jnp.where(lane8 < 64, right, jnp.where(lane8 >= 96, left, 0.0)))

    row24, lane24 = iota((24, 128), 0), iota((24, 128), 1)
    in_y = ((row24 >= 8) | (iy > 0)) & ((row24 < 16) | (iy < N - 1))
    in_z = (lane24 < 32) | ((lane24 < 64) & (iz < N - 1)) | ((lane24 >= 96) & (iz > 0))
    myz2 = jnp.where(in_y & in_z, 1.0, 0.0)
    wait(recv, 16)
    for p in range(20):
        b, q = divmod(p, 4)
        sx = [flag(ix > 1), flag(ix > 0), 1.0, flag(ix < N - 1), flag(ix < N - 2)][b]
        for by in range(3):
            v = unpack2(lambda i, j, k: rk2[i, j, k], b, q, by)
            fk2[1, 1 + p, 8 * by : 8 * by + 8, :] = v * (myz2[8 * by : 8 * by + 8] * sx)
    l2.prepare(1, 11)

    wait(recv, 4)
    wait(recv, 5)
    wait(send, 4)
    for p in range(2, 20):
        fk1[0, p] = jnp.where(lane32 < 64, fk1[0, p], ghost(s["zrf1"], (), p, 7, 8, 64))
    l1.sources(1, 11)
    l1.half("b", l1.v["b"], 2, 10)
    l1.sweep(l1.v["b"], (3, 9), (3, 9))
    l1.residual(4, 8, (8, 24), pair1)
    rf2 = s["rf2"]
    rf2[2, 1, 1] = packed2(coarse2())

    for off in wide:
        push(rf2.at[2, 1, 1], rf2.at[2 - off[0], 1 - off[1], 1 - off[2]], 6, off)
    wait(recv, 6)
    next(k_gather)
    for p in range(20):
        b, q = divmod(p, 4)
        for by in range(3):
            fk2[0, 1 + p, 8 * by : 8 * by + 8, :] = unpack2(lambda i, j, k: rf2[i, j, k], b, q, by)
    l2.sources(1, 11)
    l2.half("b", l2.v["b"], 3, 9)
    l2.sweep(l2.v["b"], (4, 8), (4, 8))
    l2.residual(5, 7, (8, 16), pair2)
    f_gather = gather(coarse3(), s["gf1"], s["gf2"], s["gf3"], 13)
    next(f_gather)
    next(f_gather)
    for _ in k_gather:
        pass
    unpack3(s["gk3"], fk3.at[1])
    l3.prepare(1, 9)
    next(f_gather)
    pair3_flat = pair3.reshape(8 * 32, 128)

    def coarse4():
        rows = row_pairs(pair3_flat, 128).reshape(8, 16, 128)
        out = None
        for h in range(2):
            into = jnp.where(lane_c == 64 * h + lane_r // 2, 0.125, 0.0)
            part = spread(rows[4 * h : 4 * h + 4].reshape(64, 128), into)
            out = part if out is None else out + part
        return out.reshape(4, 16, 128)

    for i in range(8):
        pair3[i] = fk3[1, 1 + 2 * i] + fk3[1, 2 + 2 * i]
    k4 = coarse4()
    shape4 = (4, 16, 128)
    row4, lane4 = iota(shape4, 1), iota(shape4, 2)
    z4 = lane4 & 63

    def cat(parts):
        return jnp.concatenate(parts, axis=0)

    def x_below(v):
        return cat([rotate(v[3], 64, 1)[None], v[0:3]])

    def x_above(v):
        return cat([v[1:4], rotate(v[0], 64, 1)[None]])

    def roll3(v, shift, axis):
        flat = [rotate(v[i], shift, axis)[None] for i in range(4)]
        return cat(flat)

    plane4 = iota(shape4, 0)
    first_x = (plane4 == 0) & (lane4 < 64)
    last_x = (plane4 == 3) & (lane4 >= 64)
    hs4 = 0.5 * 0.25**4
    kxl, kxu = jnp.where(first_x, 0.0, x_below(k4)), jnp.where(last_x, 0.0, x_above(k4))
    kyl = jnp.where(row4 == 0, 0.0, roll3(k4, 1, 0))
    kyu = jnp.where(row4 == 15, 0.0, roll3(k4, -1, 0))
    kzl = jnp.where(z4 == 0, 0.0, roll3(k4, 1, 1))
    kzu = jnp.where(z4 == 63, 0.0, roll3(k4, -1, 1))
    w4 = s["w4"]
    inv4 = 1.0 / (hs4 * (6.0 * k4 + kxl + kxu + kyl + kyu + kzl + kzu))
    odd4 = (plane4 + row4 + lane4) & 1
    w4[0] = jnp.where(first_x, 0.0, hs4 * (k4 + kxl))
    w4[1] = jnp.where(last_x, 0.0, hs4 * (k4 + kxu))
    w4[2] = jnp.where(row4 == 0, 0.0, hs4 * (k4 + kyl))
    w4[3] = jnp.where(row4 == 15, 0.0, hs4 * (k4 + kyu))
    w4[4] = jnp.where(z4 == 0, 0.0, hs4 * (k4 + kzl))
    w4[5] = jnp.where(z4 == 63, 0.0, hs4 * (k4 + kzu))
    w4[6] = jnp.where(odd4 == 0, inv4, 0.0)
    w4[7] = jnp.where(odd4 == 1, inv4, 0.0)

    for _ in f_gather:
        pass
    ru2 = s["ru2"]
    total = jnp.where(lane8 < 32, l2.v["b"][5, 8:16, :], 0.0)
    ru2[2, 1, 1] = total + rotate(jnp.where(lane8 < 32, l2.v["b"][6, 8:16, :], 0.0), 32, 1)
    for off in wide:
        push(ru2.at[2, 1, 1], ru2.at[2 - off[0], 1 - off[1], 1 - off[2]], 9, off)
    pack(lambda p: l1.v["b"][4 + p, 8:24, :], s["zpu1"], 4, 64)
    slabs(l1.v["b"], s["v1"], 4, 4, 3, 16, (), 7)
    edges(s["zpu1"], s["zru1"], 16, (), 8)
    s["v1"][4:8, 8:24, :] = l1.v["b"][4:8, 8:24, :]
    pack(lambda p: l0.v["b"][3 + p, 8:40, 0:128], s["zpu0"], 8, 128)
    slabs(l0.v["b"], s["v0"], 3, 8, 2, 32, (), 17)
    edges(s["zpu0"], s["zru0"], 32, (), 18)
    s["v0"][3:11, 8:40, 0:128] = l0.v["b"][3:11, 8:40, 0:128]

    unpack3(s["gf3"], fk3.at[0])
    l3.sources(1, 9)
    l3.half("b", l3.v["b"], 1, 9)
    l3.sweep(l3.v["b"], (1, 9), (1, 9))
    l3.residual(1, 9, (0, 32), pair3)
    f4 = coarse4()
    w4[8] = f4

    def around4(v):
        total = w4[0] * x_below(v) + w4[1] * x_above(v)
        total = total + (w4[2] * roll3(v, 1, 0) + w4[3] * roll3(v, -1, 0))
        return total + (w4[4] * roll3(v, 1, 1) + w4[5] * roll3(v, -1, 1))

    def bottom(i, carry):
        black = carry[1]
        red = w4[6] * (w4[8] + around4(black))
        black = w4[7] * (w4[8] + around4(red))
        return (red, black)

    zero4 = jnp.zeros(shape4, F32)
    red4, black4 = lax.fori_loop(0, BOTTOM, bottom, (zero4, zero4))
    u4 = red4 + black4

    for h in range(2):
        into = jnp.where(lane_r == 64 * h + lane_c // 2, 1.0, 0.0)
        wide4 = spread(u4.reshape(64, 128), into)
        pair3_flat[pl.ds(128 * h, 64, 2), :] = wide4
        pair3_flat[pl.ds(128 * h + 1, 64, 2), :] = wide4
    v3 = l3.v["b"]
    for j in range(1, 9):
        l3.correct(v3, j, pair3[j - 1])
    for _ in range(2):
        l3.sweep(v3, (1, 9), (1, 9))
    for j in range(1, 9):
        u3[2 + 2 * j], u3[3 + 2 * j] = l3.planes(v3, j)

    v2 = s["v2"]
    zoff = jnp.where(lane_c < 64, lane_c, lane_c - 128)
    source_lane = 16 * iz + ((zoff + 128) // 2 - 64)
    spread_z = jnp.where((lane_r == source_lane) & ((lane_c < 64) | (lane_c >= 96)), 1.0, 0.0)
    spread_y = jnp.where(iota((24, 32), 1) == 4 * iy - 4 + iota((24, 32), 0) // 2, 1.0, 0.0)
    stretched = spread(u3[pl.ds(2 * ix, 10)].reshape(320, 128), spread_z)
    side_by_side = jnp.concatenate([stretched[32 * j : 32 * j + 32] for j in range(10)], axis=1)
    corr2 = select_rows(spread_y, side_by_side)
    wait(recv, 9)
    for j in range(1, 11):
        b, q = divmod(j - 1, 2)
        for by in range(3):
            v2[j, 8 * by : 8 * by + 8, :] = unpack2(lambda i, j, k: ru2[i, j, k], b, q, by)
        l2.correct(v2, j, corr2[:, 128 * (j - 1) : 128 * j])
    l2.sweep(v2, (2, 10), (2, 10))
    l2.sweep(v2, (3, 9), (3, 9))

    spread1 = jnp.where(lane_r == jnp.where(lane_c >= 96, 64 + lane_c // 2, lane_c // 2), 1.0, 0.0)
    up1 = s["up1"]
    coarse = []
    for j in range(3, 9):
        coarse += list(l2.planes(v2, j))
    up1[...] = spread(jnp.concatenate(coarse[1:11], axis=0), spread1).reshape(10, 24, 128)
    tall1 = s["tall1"]
    wait(recv, 7)
    wait(recv, 8)
    v1 = s["v1"]
    for j in range(1, 11):
        v1[j] = jnp.where(lane32 < 64, v1[j], ghost(s["zru1"], (), j, 4, 4, 64))
        part = up1[j - 1, 4:20, :]
        tall1[j - 1, pl.ds(0, 16, 2), :] = part
        tall1[j - 1, pl.ds(1, 16, 2), :] = part
        l1.correct(v1, j, tall1[j - 1])
    l1.sweep(v1, (1, 11), (2, 10))
    l1.sweep(v1, (2, 10), (3, 9))

    spread0 = jnp.where(iota((128, 256), 0) == iota((128, 256), 1) // 2, 1.0, 0.0)
    up0, tall0 = s["up0"], s["tall0"]
    coarse = []
    for j in range(3, 9):
        coarse += list(l1.planes(v1, j))
    up0[...] = spread(jnp.concatenate(coarse, axis=0), spread0).reshape(12, 32, 256)
    wait(recv, 17)
    wait(recv, 18)
    v0 = s["v0"]
    for j in range(1, 13):
        v0[j, :, 128:256] = ghost(s["zru0"], (), j, 3, 8, 0)
        for t in range(2):
            lanes = slice(128 * t, 128 * t + 128)
            part = up0[j - 1, 4:28, lanes]
            tall0[j - 1, t, pl.ds(0, 24, 2), :] = part
            tall0[j - 1, t, pl.ds(1, 24, 2), :] = part
            black = l0.i["b"][j, :, lanes] > 0.0
            v0[j, :, lanes] = jnp.where(black, v0[j, :, lanes] + tall0[j - 1, t], 0.0)
    l0.sweep(v0, (1, 13), (2, 12))
    l0.sweep(v0, (2, 12), (3, 11))
    for j in range(3, 11):
        a, b = l0.planes(v0, j)
        out_ref[2 * j - 6] = a[8:40, 0:128]
        out_ref[2 * j - 5] = b[8:40, 0:128]
    for sem in sorted(sent):
        if sem not in (0, 2, 4):
            wait(send, sem)


def vmem(*shape):
    return pltpu.VMEM(shape, F32)


def scratch_shapes():
    shapes = {}
    sizes = [(26, 12, 48, 256), (22, 10, 32, 128), (22, 10, 24, 128), (18, 8, 32, 128)]
    for no, (planes, pairs, rows, lanes) in enumerate(sizes):
        shapes[f"fk{no}"] = vmem(2, planes, rows, lanes)
        names = ["xin", "dr", "db"] + [n + c for n in ("v", "xo", "wy", "wz", "inv", "src") for c in "rb"]
        for name in names + (["v"] if no < 3 else []):
            shapes[f"{name}{no}"] = vmem(pairs + 2, rows, lanes)
    shapes["zp0"], shapes["zr0"] = vmem(2, 2, 32, 128), vmem(2, 3, 2, 48, 128)
    shapes["ze0"], shapes["zs0"] = vmem(2, 32, 128), vmem(2, 3, 48, 128)
    shapes["zpu0"], shapes["zru0"] = vmem(2, 32, 128), vmem(2, 3, 48, 128)
    for name in ("k1", "f1", "pu1"):
        shapes["z" + name] = vmem(2, 16, 128)
    for name in ("zrk1", "zrf1", "zru1"):
        shapes[name] = vmem(2, 3, 32, 128)
    for name in ("rk2", "rf2", "ru2"):
        shapes[name] = vmem(5, 3, 3, 8, 128)
    for name in "kf":
        shapes[f"g{name}1"] = vmem(8, 8, 128)
        shapes[f"g{name}2"] = vmem(8, 2, 8, 128)
        shapes[f"g{name}3"] = vmem(8, 2, 4, 8, 128)
    shapes["pair0"], shapes["pair1"] = vmem(8, 32, 128), vmem(4, 16, 128)
    shapes["pair2"], shapes["pair3"] = vmem(2, 8, 128), vmem(8, 32, 128)
    shapes["w4"], shapes["u3"] = vmem(9, 4, 16, 128), vmem(24, 32, 128)
    shapes["up0"], shapes["tall0"] = vmem(12, 32, 256), vmem(12, 2, 48, 128)
    shapes["up1"], shapes["tall1"] = vmem(10, 24, 128), vmem(10, 32, 128)
    shapes["dummy"] = vmem(256, 8, 128)
    shapes["send"] = pltpu.SemaphoreType.DMA((20,))
    shapes["recv"] = pltpu.SemaphoreType.DMA((20,))
    shapes["load"] = pltpu.SemaphoreType.DMA((2,))
    return shapes


SCRATCH = scratch_shapes()


def on_device(source_term, conductivity):
    return pl.pallas_call(
        kernel,
        out_shape=jax.ShapeDtypeStruct((16, 32, 128), F32),
        in_specs=[pl.BlockSpec(memory_space=pl.ANY)] * 2,
        out_specs=pl.BlockSpec(memory_space=pltpu.VMEM),
        scratch_shapes=list(SCRATCH.values()),
        compiler_params=pltpu.CompilerParams(
            collective_id=0, has_side_effects=True, vmem_limit_bytes=60 * 2**20
        ),
        name="vcycle",
    )(source_term, conductivity)


def solution(mesh):
    spec = P("gx", "gy", "gz")
    return jax.shard_map(
        on_device, mesh=mesh, in_specs=(spec, spec), out_specs=spec, check_vma=False
    )
```

time: 103 us -> 71.9 us (0.70)
  Pallas kernels: 101 us -> 70.1 us
    pallas_call x1, Pallas kernels: 101 us -> 70.1 us  [on_device(): pl.pallas_call(kernel, out_shape=jax.ShapeDtypeStruct((16, 32, 128), F32)...]
    unnamed x5 -> x1, local copies, waits for them, and re-layouts: 2.6 us -> 1.67 us
where the time goes in v2:
time: 71.9 us; the launch traced here: 71.8 us
  Pallas kernels  70.1 us (97%)
  local copies, waits for them, and re-layouts  1.67 us (2%)
    pallas_call x1, Pallas kernels, on_device(): pl.pallas_call(kernel, out_shape=jax.ShapeDtypeStruct((16, 32, 128), F32)...  70.1 us
    unnamed x1, local copies, waits for them, and re-layouts  1.67 us

profile of v2, /device:TPU:1, one launch (start us, length us, event | category | flops | bytes accessed | tf_op | source)
XLA Modules:
  0.0 71.8 jit_solution(14222615567944477196)
XLA Ops:
  0.0 70.1 %vcycle.1 = f32[16,32,128]{2,1,0:T(8,128)} custom-call(f32[16,32,128]{2,1,0:T(8,128)} %f_hbm.1, f32[16,32,128]{2,1,0:T(8,128)} %k_hbm.1), custom_call_target="tpu_custom_call" | custom-call | tf_op jit(solution)/shard_map/vcycle/pallas_call | solution.py:699
  70.1 1.7 %copy.4 = f32[16,32,128]{2,1,0:T(8,128)} copy(f32[16,32,128]{2,1,0:T(8,128)} %vcycle.1) | data formatting | bytes 524288

commit v3 on v2

--- a/solution.py
+++ b/solution.py
@@ -45,7 +45,7 @@
 
 
 class Level:
-    def __init__(self, s, no, fk, scale, closed, block):
+    def __init__(self, s, no, fk, scale, closed, block, steps=None):
         self.f, self.k = fk.at[0], fk.at[1]
         self.xin, self.dr, self.db = s[f"xin{no}"], s[f"dr{no}"], s[f"db{no}"]
         self.v = {"r": s[f"vr{no}"], "b": s[f"vb{no}"]}
@@ -53,11 +53,28 @@
             {c: s[f"{n}{c}{no}"] for c in "rb"} for n in ("xo", "wy", "wz", "inv", "src")
         )
         self.pairs, self.rows, self.lanes = self.xin.shape
-        self.scale, self.closed, self.block = (scale, closed, block)
+        self.scale, self.closed, self.block, self.steps = (scale, closed, block, steps)
 
     def even(self):
         shape = (self.rows, self.lanes)
-        return (iota(shape, 0) + iota(shape, 1)) & 1 == 0
+        row = iota(shape, 0) if self.steps is None else iota(shape, 0) // 8
+        return (row + iota(shape, 1)) & 1 == 0
+
+    def read(self, ref, p):
+        if self.steps is None:
+            return ref[p]
+        tiles = []
+        for t in range(0, self.lanes, 128):
+            rows = [ref[t // 128, p, pl.ds(r, 8, self.steps), :] for r in range(self.steps)]
+            tiles.append(jnp.concatenate(rows, axis=0))
+        return jnp.concatenate(tiles, axis=1)
+
+    def shift(self, a, way):
+        if self.steps is None:
+            return rotate(a, way, 0)
+        if way == 1:
+            return jnp.concatenate([rotate(a[self.rows - 8 :], 1, 0), a[: self.rows - 8]], axis=0)
+        return jnp.concatenate([a[8:], rotate(a[:8], -1, 0)], axis=0)
 
     def loop(self, lo, hi, body):
         block = min(self.block, hi - lo)
@@ -75,13 +92,12 @@
         for j in range(lo + (hi - lo) // block * block, hi):
             body(j)
 
-    def prepare(self, lo, hi, sources=True):
+    def prepare(self, lo, hi):
         shape = (self.rows, self.lanes)
         hs = 0.5 * self.scale
 
-        def one(p):
-            k = self.k[p]
-            kyl, kyu = rotate(k, 1, 0), rotate(k, -1, 0)
+        def one(before, k, after):
+            kyl, kyu = self.shift(k, 1), self.shift(k, -1)
             kzl, kzu = rotate(k, 1, 1), rotate(k, -1, 1)
             wy, wz = hs * (k + kyl), hs * (k + kzl)
             if self.closed:
@@ -92,18 +108,18 @@
                 kzu = jnp.where(lane == self.lanes - 1, 0.0, kzu)
                 wy = jnp.where(row == 0, 0.0, wy)
                 wz = jnp.where(lane == 0, 0.0, wz)
-            diag = hs * (6.0 * k + self.k[p - 1] + self.k[p + 1] + kyl + kyu + kzl + kzu)
+            diag = hs * (6.0 * k + before + after + kyl + kyu + kzl + kzu)
             inside = k > 0.0
             inv = jnp.where(inside, 1.0 / jnp.where(inside, diag, 1.0), 0.0)
             return wy, wz, inv, diag
 
         def body(j):
             even = self.even()
-            p = 2 * j - 1
-            first, second = one(p), one(p + 1)
-            below = hs * (self.k[p] + self.k[p - 1])
-            above = hs * (self.k[p + 2] + self.k[p + 1])
-            self.xin[j] = hs * (self.k[p] + self.k[p + 1])
+            k = [self.read(self.k, 2 * j - 2 + n) for n in range(4)]
+            first, second = one(k[0], k[1], k[2]), one(k[1], k[2], k[3])
+            below = hs * (k[0] + k[1])
+            above = hs * (k[2] + k[3])
+            self.xin[j] = hs * (k[1] + k[2])
             self.xo["r"][j] = jnp.where(even, below, above)
             self.xo["b"][j] = jnp.where(even, above, below)
             for ref, n in ((self.y, 0), (self.z, 1), (self.i, 2)):
@@ -117,7 +133,7 @@
     def sources(self, lo, hi):
         def body(j):
             even = self.even()
-            a, b = self.f[2 * j - 1], self.f[2 * j]
+            a, b = self.read(self.f, 2 * j - 1), self.read(self.f, 2 * j)
             red = jnp.where(even, a, b)
             self.g["r"][j] = red
             self.g["b"][j] = jnp.where(even, b, a)
@@ -131,14 +147,17 @@
         if colour == "b":
             before, after = after, before
         total = self.xin[j] * u + self.xo[colour][j] * jnp.where(self.even(), before, after)
-        total = total + (self.y[colour][j] * rotate(u, 1, 0) + rotate(self.y[far][j] * u, -1, 0))
+        total = total + (self.y[colour][j] * self.shift(u, 1) + self.shift(self.y[far][j] * u, -1))
         return total + (self.z[colour][j] * rotate(u, 1, 1) + rotate(self.z[far][j] * u, -1, 1))
+
+    def updated(self, colour, other, j):
+        return self.i[colour][j] * (self.g[colour][j] + self.around(colour, other, j))
 
     def half(self, colour, black, lo, hi):
         target, other = (self.v["r"], black) if colour == "r" else (black, self.v["r"])
 
         def body(j):
-            target[j] = self.i[colour][j] * (self.g[colour][j] + self.around(colour, other, j))
+            target[j] = self.updated(colour, other, j)
 
         self.loop(lo, hi, body)
 
@@ -151,7 +170,13 @@
             r, b = self.v["r"], self.v["b"]
             red = self.g["r"][j] - (self.dr[j] * r[j] - self.around("r", b, j))
             black = self.g["b"][j] - (self.db[j] * b[j] - self.around("b", r, j))
-            out[j - lo] = (red + black)[rows[0] : rows[1], 0:128]
+            both = (red + black)[:, 0:128]
+            if self.steps is None:
+                out[j - lo] = both[rows[0] : rows[1]]
+                return
+            for t in range(0, self.steps, 2):
+                two = both[8 * t : 8 * t + 8] + both[8 * t + 8 : 8 * t + 16]
+                out[j - lo, pl.ds(t // 2, 8, self.steps // 2), :] = two
 
         self.loop(lo, hi, body)
 
@@ -195,10 +220,10 @@
 
     fk0, fk1, fk2, fk3 = s["fk0"], s["fk1"], s["fk2"], s["fk3"]
 
-    l0, l1 = Level(s, 0, fk0, 1.0, False, 2), Level(s, 1, fk1, 0.25, False, 12)
+    l0, l1 = Level(s, 0, fk0, 1.0, False, 2, 6), Level(s, 1, fk1, 0.25, False, 12)
     l2, l3 = Level(s, 2, fk2, 0.25**2, False, 12), Level(s, 3, fk3, 0.25**3, True, 12)
 
-    own0 = [fk0.at[a, pl.ds(5, 16), pl.ds(8, 32), pl.ds(0, 128)] for a in range(2)]
+    own0 = [fk0.at[a, 0, pl.ds(5, 16), pl.ds(8, 32)] for a in range(2)]
     loads = [pltpu.make_async_copy(r, own0[a], s["load"].at[a]) for a, r in enumerate((f_hbm, k_hbm))]
     for c in loads:
         c.start()
@@ -219,12 +244,11 @@
     def pack(own, zp, planes, length):
         left = right = None
         for p in range(planes):
-            v = own(p)
-            group = iota(v.shape, 1) // 8 == p
-            a, b = rotate(v, 8 * p, 1), rotate(v, 8 * p - (length - 8), 1)
-            left = a if p == 0 else jnp.where(group, a, left)
-            right = b if p == 0 else jnp.where(group, b, right)
-        zp[0], zp[1] = left, right
+            v = rotate(own(p), 8 * p, 1)
+            group = iota(v.shape, 1) // 8
+            left = v if p == 0 else jnp.where(group == p, v, left)
+            right = v if p == 0 else jnp.where(group == (p + length // 8 - 1) % 16, v, right)
+        zp[0], zp[1] = left, rotate(right, 8 - length, 1)
 
     def slabs(src, dst, start, nx, w, ny, lead, sem, corners=None):
         for sx in (-1, 0, 1):
@@ -273,11 +297,11 @@
         return flag(ix > 0) if p < h else flag(ix < N - 1) if p >= h + nx else 1.0
 
     zp0, ze0, zr0, zs0 = s["zp0"], s["ze0"], s["zr0"], s["zs0"]
+    slabs(fk0, fk0, 5, 16, 4, 32, (slice(None), 0), 0)
+    for sx, a, b in ((1, 16, 0), (-1, 9, 25)):
+        push(fk0.at[1, 0, a, pl.ds(8, 32)], fk0.at[1, 0, b, pl.ds(8, 32)], 0, (sx, 0, 0))
     for a in range(2):
-        pack(lambda p, a=a: fk0[a, 5 + p, 8:40, 0:128], zp0.at[:, a], 16, 128)
-    slabs(fk0, fk0, 5, 16, 4, 32, (slice(None),), 0)
-    for sx, a, b in ((1, 16 + 0, 0), (-1, 9, 25)):
-        push(fk0.at[1, a, pl.ds(8, 32), pl.ds(0, 128)], fk0.at[1, b, pl.ds(8, 32), pl.ds(0, 128)], 0, (sx, 0, 0))
+        pack(lambda p, a=a: fk0[a, 0, 5 + p, 8:40, :], zp0.at[:, a], 16, 128)
     edges(zp0, zr0, 32, (slice(None),), 1, (0,))
     lane32 = iota((32, 128), 1)
     for side in range(2):
@@ -299,11 +323,11 @@
     halve1 = jnp.where((lane_r // 2 == lane_c), 0.125, 0.0)
     halve2 = jnp.where((lane_r // 2 == lane_c) & (lane_c < 32), 0.125, 0.0)
 
+    pairk = s["pairk"]
     pair0, pair1, pair2, pair3 = s["pair0"], s["pair1"], s["pair2"], s["pair3"]
 
-    def coarse1():
-        flat = pair0.reshape(256, 128)
-        return spread(row_pairs(flat, 128), halve1).reshape(8, 16, 128)
+    def coarse1(rows):
+        return spread(rows, halve1).reshape(8, 16, 128)
 
     def coarse2():
         flat = pair1.reshape(64, 128)
@@ -351,15 +375,20 @@
         group = iota((32, 128), 1) // 16
         for h in range(2):
             blocks = [g3[j, h].reshape(32, 128) for j in range(8)]
+            for bit in (4, 2, 1):
+                low = group & bit == 0
+                for j in range(8):
+                    if j & bit:
+                        continue
+                    a, c = blocks[j], blocks[j + bit]
+                    blocks[j] = jnp.where(low, a, rotate(c, 16 * bit, 1))
+                    blocks[j + bit] = jnp.where(low, rotate(a, -16 * bit, 1), c)
             for g in range(8):
-                total = rotate(blocks[0], 16 * (0 - g), 1)
-                for j in range(1, 8):
-                    total = jnp.where(group == j, rotate(blocks[j], 16 * (j - g), 1), total)
-                out[1 + 8 * h + g] = total
+                out[1 + 8 * h + g] = blocks[g]
 
     for i in range(8):
-        pair0[i] = fk0[1, 5 + 2 * i, 8:40, 0:128] + fk0[1, 6 + 2 * i, 8:40, 0:128]
-    k1_own = coarse1()
+        pairk[i] = fk0[1, 0, 5 + 2 * i, 8:40, :] + fk0[1, 0, 6 + 2 * i, 8:40, :]
+    k1_own = coarse1(row_pairs(pairk.reshape(256, 128), 128))
     fk1[1, 7:15, 8:24, :] = k1_own
     for i in range(4):
         pair1[i] = k1_own[2 * i] + k1_own[2 * i + 1]
@@ -383,6 +412,8 @@
     for p in (0, 21):
         fk1[1, p] = jnp.zeros((32, 128), F32)
         fk2[1, p] = jnp.zeros((24, 128), F32)
+    for j in (1, 2, 9, 10):
+        l2.v["r"][j] = jnp.zeros((24, 128), F32)
     for p in (1, 20):
         fk1[0, p] = jnp.zeros((32, 128), F32)
     for p in (0, 17):
@@ -394,11 +425,11 @@
     wait(recv, 0)
     wait(recv, 1)
     wait(send, 0)
+    next(k_gather)
     slabs(fk1, fk1, 7, 8, 6, 16, (1,), 2)
     edges(s["zk1"], s["zrk1"], 16, (), 3)
     for off in wide:
         push(rk2.at[2, 1, 1], rk2.at[2 - off[0], 1 - off[1], 1 - off[2]], 16, off)
-    next(k_gather)
     myz0 = inside_yz(48, 32, 128, 192, 256)
     row48 = iota((48, 128), 0)
     for p in range(26):
@@ -406,22 +437,22 @@
             g = ghost0(a, p)
             if a == 1:
                 sx = inside_x(p, 5, 16)
-                main = fk0[1, p, :, 0:128] * (myz0[:, 0:128] * sx)
+                main = fk0[1, 0, p] * (myz0[:, 0:128] * sx)
                 if not 0 < p < 25:
                     main = jnp.where((row48 >= 8) & (row48 < 40), main, 0.0)
-                fk0[1, p, :, 0:128] = main
+                fk0[1, 0, p] = main
                 g = g * (myz0[:, 128:256] * sx)
-            fk0[a, p, :, 128:256] = g
+            fk0[a, 1, p] = g
     l0.prepare(1, 13)
     l0.sources(1, 13)
     l0.half("b", l0.v["b"], 1, 13)
     l0.sweep(l0.v["b"], (2, 12), (2, 12))
     l0.residual(3, 11, (8, 40), pair0)
-    f1_own = coarse1()
+    f1_own = coarse1(pair0[:, 4:20, :].reshape(128, 128))
     fk1[0, 7:15, 8:24, :] = f1_own
 
+    slabs(fk1, fk1, 7, 8, 5, 16, (0,), 4)
     pack(lambda p: fk1[0, 7 + p, 8:24, :], s["zf1"], 8, 64)
-    slabs(fk1, fk1, 7, 8, 5, 16, (0,), 4)
     edges(s["zf1"], s["zrf1"], 16, (), 5)
     wait(recv, 2)
     wait(recv, 3)
@@ -466,26 +497,51 @@
     rf2 = s["rf2"]
     rf2[2, 1, 1] = packed2(coarse2())
 
-    for off in wide:
-        push(rf2.at[2, 1, 1], rf2.at[2 - off[0], 1 - off[1], 1 - off[2]], 6, off)
+    far = [off for off in wide if off not in near]
+    for sem, group in ((6, near), (19, far)):
+        for off in group:
+            push(rf2.at[2, 1, 1], rf2.at[2 - off[0], 1 - off[1], 1 - off[2]], sem, off)
+
+    def source2(boxes):
+        for b in boxes:
+            for p in range(4 * b, 4 * b + 4):
+                for by in range(3):
+                    fk2[0, 1 + p, 8 * by : 8 * by + 8, :] = unpack2(lambda i, j, k: rf2[i, j, k], b, p % 4, by)
+            l2.sources(1 + 2 * b, 3 + 2 * b)
+
     wait(recv, 6)
     next(k_gather)
-    for p in range(20):
-        b, q = divmod(p, 4)
-        for by in range(3):
-            fk2[0, 1 + p, 8 * by : 8 * by + 8, :] = unpack2(lambda i, j, k: rf2[i, j, k], b, q, by)
-    l2.sources(1, 11)
+    source2((1, 2, 3))
     l2.half("b", l2.v["b"], 3, 9)
     l2.sweep(l2.v["b"], (4, 8), (4, 8))
     l2.residual(5, 7, (8, 16), pair2)
     f_gather = gather(coarse3(), s["gf1"], s["gf2"], s["gf3"], 13)
     next(f_gather)
+    slabs(l1.v["b"], s["v1"], 4, 4, 3, 16, (), 7)
+    pack(lambda p: l1.v["b"][4 + p, 8:24, :], s["zpu1"], 4, 64)
+    edges(s["zpu1"], s["zru1"], 16, (), 8)
+    s["v1"][4:8, 8:24, :] = l1.v["b"][4:8, 8:24, :]
+    vb0n, v0n = s["vb0n"], s["v0n"]
+    for j in range(3, 11):
+        for t in range(6):
+            vb0n[j, pl.ds(t, 8, 6), :] = l0.v["b"][j, 8 * t : 8 * t + 8, 0:128]
+    pack(lambda p: vb0n[3 + p, 8:40, :], s["zpu0"], 8, 128)
+    v0n[0, 3:11, 8:40, :] = vb0n[3:11, 8:40, :]
     next(f_gather)
+    slabs(vb0n, v0n.at[0], 3, 8, 2, 32, (), 17)
+    edges(s["zpu0"], s["zru0"], 32, (), 18)
+    wait(recv, 19)
+    source2((0, 4))
     for _ in k_gather:
         pass
     unpack3(s["gk3"], fk3.at[1])
     l3.prepare(1, 9)
     next(f_gather)
+    ru2 = s["ru2"]
+    total = jnp.where(lane8 < 32, l2.v["b"][5, 8:16, :], 0.0)
+    ru2[2, 1, 1] = total + rotate(jnp.where(lane8 < 32, l2.v["b"][6, 8:16, :], 0.0), 32, 1)
+    for off in wide:
+        push(ru2.at[2, 1, 1], ru2.at[2 - off[0], 1 - off[1], 1 - off[2]], 9, off)
     pair3_flat = pair3.reshape(8 * 32, 128)
 
     def coarse4():
@@ -540,20 +596,6 @@
 
     for _ in f_gather:
         pass
-    ru2 = s["ru2"]
-    total = jnp.where(lane8 < 32, l2.v["b"][5, 8:16, :], 0.0)
-    ru2[2, 1, 1] = total + rotate(jnp.where(lane8 < 32, l2.v["b"][6, 8:16, :], 0.0), 32, 1)
-    for off in wide:
-        push(ru2.at[2, 1, 1], ru2.at[2 - off[0], 1 - off[1], 1 - off[2]], 9, off)
-    pack(lambda p: l1.v["b"][4 + p, 8:24, :], s["zpu1"], 4, 64)
-    slabs(l1.v["b"], s["v1"], 4, 4, 3, 16, (), 7)
-    edges(s["zpu1"], s["zru1"], 16, (), 8)
-    s["v1"][4:8, 8:24, :] = l1.v["b"][4:8, 8:24, :]
-    pack(lambda p: l0.v["b"][3 + p, 8:40, 0:128], s["zpu0"], 8, 128)
-    slabs(l0.v["b"], s["v0"], 3, 8, 2, 32, (), 17)
-    edges(s["zpu0"], s["zru0"], 32, (), 18)
-    s["v0"][3:11, 8:40, 0:128] = l0.v["b"][3:11, 8:40, 0:128]
-
     unpack3(s["gf3"], fk3.at[0])
     l3.sources(1, 9)
     l3.half("b", l3.v["b"], 1, 9)
@@ -627,29 +669,37 @@
     l1.sweep(v1, (2, 10), (3, 9))
 
     spread0 = jnp.where(iota((128, 256), 0) == iota((128, 256), 1) // 2, 1.0, 0.0)
-    up0, tall0 = s["up0"], s["tall0"]
+    up0 = s["up0"]
     coarse = []
     for j in range(3, 9):
         coarse += list(l1.planes(v1, j))
-    up0[...] = spread(jnp.concatenate(coarse, axis=0), spread0).reshape(12, 32, 256)
+    wide0 = spread(jnp.concatenate(coarse, axis=0), spread0).reshape(12, 32, 256)
+    up0[0], up0[1] = wide0[:, :, 0:128], wide0[:, :, 128:256]
     wait(recv, 17)
     wait(recv, 18)
     v0 = s["v0"]
     for j in range(1, 13):
-        v0[j, :, 128:256] = ghost(s["zru0"], (), j, 3, 8, 0)
+        v0n[1, j] = ghost(s["zru0"], (), j, 3, 8, 0)
+    for j in range(1, 13):
+        tiles = []
         for t in range(2):
-            lanes = slice(128 * t, 128 * t + 128)
-            part = up0[j - 1, 4:28, lanes]
-            tall0[j - 1, t, pl.ds(0, 24, 2), :] = part
-            tall0[j - 1, t, pl.ds(1, 24, 2), :] = part
-            black = l0.i["b"][j, :, lanes] > 0.0
-            v0[j, :, lanes] = jnp.where(black, v0[j, :, lanes] + tall0[j - 1, t], 0.0)
+            rows = [up0[t, j - 1, pl.ds(4 + c, 8, 3), :] for c in range(3)]
+            tiles.append(jnp.concatenate([rows[c // 2] for c in range(6)], axis=0))
+        corr = jnp.concatenate(tiles, axis=1)
+        v0[j] = jnp.where(l0.i["b"][j] > 0.0, l0.read(v0n, j) + corr, 0.0)
     l0.sweep(v0, (1, 13), (2, 12))
-    l0.sweep(v0, (2, 12), (3, 11))
-    for j in range(3, 11):
-        a, b = l0.planes(v0, j)
-        out_ref[2 * j - 6] = a[8:40, 0:128]
-        out_ref[2 * j - 5] = b[8:40, 0:128]
+    l0.half("r", v0, 2, 12)
+    outn = s["outn"]
+
+    def last(j):
+        black = l0.updated("b", l0.v["r"], j)
+        red, even = l0.v["r"][j], l0.even()
+        for n, plane in enumerate((jnp.where(even, red, black), jnp.where(even, black, red))):
+            for t in range(6):
+                outn[2 * j - 6 + n, pl.ds(t, 8, 6), :] = plane[8 * t : 8 * t + 8, 0:128]
+
+    l0.loop(3, 11, last)
+    out_ref[...] = outn[:, 8:40, :]
     for sem in sorted(sent):
         if sem not in (0, 2, 4):
             wait(send, sem)
@@ -663,7 +713,7 @@
     shapes = {}
     sizes = [(26, 12, 48, 256), (22, 10, 32, 128), (22, 10, 24, 128), (18, 8, 32, 128)]
     for no, (planes, pairs, rows, lanes) in enumerate(sizes):
-        shapes[f"fk{no}"] = vmem(2, planes, rows, lanes)
+        shapes[f"fk{no}"] = vmem(2, 2, planes, rows, 128) if no == 0 else vmem(2, planes, rows, lanes)
         names = ["xin", "dr", "db"] + [n + c for n in ("v", "xo", "wy", "wz", "inv", "src") for c in "rb"]
         for name in names + (["v"] if no < 3 else []):
             shapes[f"{name}{no}"] = vmem(pairs + 2, rows, lanes)
@@ -680,10 +730,12 @@
         shapes[f"g{name}1"] = vmem(8, 8, 128)
         shapes[f"g{name}2"] = vmem(8, 2, 8, 128)
         shapes[f"g{name}3"] = vmem(8, 2, 4, 8, 128)
-    shapes["pair0"], shapes["pair1"] = vmem(8, 32, 128), vmem(4, 16, 128)
+    shapes["pair0"], shapes["pair1"] = vmem(8, 24, 128), vmem(4, 16, 128)
+    shapes["pairk"], shapes["outn"] = vmem(8, 32, 128), vmem(16, 48, 128)
+    shapes["vb0n"], shapes["v0n"] = vmem(14, 48, 128), vmem(2, 14, 48, 128)
     shapes["pair2"], shapes["pair3"] = vmem(2, 8, 128), vmem(8, 32, 128)
     shapes["w4"], shapes["u3"] = vmem(9, 4, 16, 128), vmem(24, 32, 128)
-    shapes["up0"], shapes["tall0"] = vmem(12, 32, 256), vmem(12, 2, 48, 128)
+    shapes["up0"] = vmem(2, 12, 32, 128)
     shapes["up1"], shapes["tall1"] = vmem(10, 24, 128), vmem(10, 32, 128)
     shapes["dummy"] = vmem(256, 8, 128)
     shapes["send"] = pltpu.SemaphoreType.DMA((20,))
@@ -703,7 +755,7 @@
         out_specs=pl.BlockSpec(memory_space=pltpu.VMEM),
         scratch_shapes=list(SCRATCH.values()),
         compiler_params=pltpu.CompilerParams(
-            collective_id=0, has_side_effects=True, vmem_limit_bytes=60 * 2**20
+            collective_id=0, has_side_effects=True, vmem_limit_bytes=107 * 2**19
         ),
         name="vcycle",
     )(source_term, conductivity)

time: 71.9 us -> 67.8 us (0.943)
  Pallas kernels: 70.1 us -> 66.9 us
  local copies, waits for them, and re-layouts: 1.67 us -> 0.71 us
    pallas_call x1, Pallas kernels: 70.1 us -> 66.9 us  [on_device(): pl.pallas_call(kernel, out_shape=jax.ShapeDtypeStruct((16, 32, 128), F32)...]
    unnamed x1, local copies, waits for them, and re-layouts: 1.67 us -> 0.71 us
where the time goes in v3:
time: 67.8 us; the launch traced here: 67.7 us
  Pallas kernels  66.9 us (99%)
  local copies, waits for them, and re-layouts  0.71 us (1%)
    pallas_call x1, Pallas kernels, on_device(): pl.pallas_call(kernel, out_shape=jax.ShapeDtypeStruct((16, 32, 128), F32)...  66.9 us

profile of v3, /device:TPU:1, one launch (start us, length us, event | category | flops | bytes accessed | tf_op | source)
XLA Modules:
  0.0 67.7 jit_solution(4365119103977039987)
XLA Ops:
  0.0 66.9 %vcycle.1 = f32[16,32,128]{2,1,0:T(8,128)S(1)} custom-call(f32[16,32,128]{2,1,0:T(8,128)} %f_hbm.1, f32[16,32,128]{2,1,0:T(8,128)} %k_hbm.1), custom_call_target="tpu_custom_call" | custom-call | tf_op jit(solution)/shard_map/vcycle/pallas_call | solution.py:751
  67.0 0.7 %copy.4 = f32[16,32,128]{2,1,0:T(8,128)} copy(f32[16,32,128]{2,1,0:T(8,128)S(1)} %vcycle.1) | data formatting | bytes 524288

commit v4 on v3

--- a/solution.py
+++ b/solution.py
@@ -220,7 +220,7 @@
 
     fk0, fk1, fk2, fk3 = s["fk0"], s["fk1"], s["fk2"], s["fk3"]
 
-    l0, l1 = Level(s, 0, fk0, 1.0, False, 2, 6), Level(s, 1, fk1, 0.25, False, 12)
+    l0, l1 = Level(s, 0, fk0, 1.0, False, 12, 6), Level(s, 1, fk1, 0.25, False, 12)
     l2, l3 = Level(s, 2, fk2, 0.25**2, False, 12), Level(s, 3, fk3, 0.25**3, True, 12)
 
     own0 = [fk0.at[a, 0, pl.ds(5, 16), pl.ds(8, 32)] for a in range(2)]
@@ -248,7 +248,7 @@
             group = iota(v.shape, 1) // 8
             left = v if p == 0 else jnp.where(group == p, v, left)
             right = v if p == 0 else jnp.where(group == (p + length // 8 - 1) % 16, v, right)
-        zp[0], zp[1] = left, rotate(right, 8 - length, 1)
+        zp[0], zp[1] = left, right
 
     def slabs(src, dst, start, nx, w, ny, lead, sem, corners=None):
         for sx in (-1, 0, 1):
@@ -271,18 +271,17 @@
                     b = (1 - side, 1 - sx) + lead + (pl.ds(ys[2], ys[1]),)
                     push(zp.at[a], zr.at[b], sem, (sx, sy, sz))
 
-    def place(right, left, base):
+    def place(right, left, at, base):
         lane = iota(right.shape, 1)
-        return jnp.where((lane >= base) & (lane < base + 8), right, jnp.where(lane >= 120, left, 0.0))
+        both = rotate(jnp.where(lane // 8 == at, right, left), base - 8 * at, 1)
+        return jnp.where((lane >= base) & (lane < base + 8) | (lane >= 120), both, 0.0)
 
     def slot(p, start, nx):
         return (0, p - start + nx) if p < start else (1, p - start) if p < start + nx else (2, p - start - nx)
 
     def ghost(zr, lead, p, start, nx, base):
         b, q = slot(p, start, nx)
-        right = rotate(zr[(1, b) + lead], base - 8 * q, 1)
-        left = rotate(zr[(0, b) + lead], 120 - 8 * q, 1)
-        return place(right, left, base)
+        return place(zr[(1, b) + lead], zr[(0, b) + lead], q, base)
 
     def flag(condition):
         return jnp.where(condition, 1.0, 0.0)
@@ -297,18 +296,21 @@
         return flag(ix > 0) if p < h else flag(ix < N - 1) if p >= h + nx else 1.0
 
     zp0, ze0, zr0, zs0 = s["zp0"], s["ze0"], s["zr0"], s["zs0"]
-    slabs(fk0, fk0, 5, 16, 4, 32, (slice(None), 0), 0)
+    slabs(fk0, fk0, 5, 16, 4, 32, (1, 0), 0)
     for sx, a, b in ((1, 16, 0), (-1, 9, 25)):
         push(fk0.at[1, 0, a, pl.ds(8, 32)], fk0.at[1, 0, b, pl.ds(8, 32)], 0, (sx, 0, 0))
-    for a in range(2):
+    for a in (1, 0):
         pack(lambda p, a=a: fk0[a, 0, 5 + p, 8:40, :], zp0.at[:, a], 16, 128)
-    edges(zp0, zr0, 32, (slice(None),), 1, (0,))
     lane32 = iota((32, 128), 1)
     for side in range(2):
-        fs, ks = zp0[side, 0], zp0[side, 1]
+        fs, ks = [rotate(zp0[side, a], 8 * side, 1) for a in range(2)]
         v = jnp.where(lane32 < 32, fs, rotate(fs, -64, 1))
-        ze0[side] = jnp.where(lane32 < 64, v, jnp.where(lane32 < 96, rotate(ks, 64, 1), ks))
+        v = jnp.where(lane32 < 64, v, jnp.where(lane32 < 96, rotate(ks, 64, 1), ks))
+        ze0[side] = rotate(v, -8 * side, 1)
+    edges(zp0, zr0, 32, (1,), 1, (0,))
     edges(ze0, zs0, 32, (), 1, (-1, 1))
+    slabs(fk0, fk0, 5, 16, 4, 32, (0, 0), 20)
+    edges(zp0, zr0, 32, (0,), 21, (0,))
 
     def ghost0(a, p):
         b, q = slot(p, 5, 16)
@@ -316,8 +318,7 @@
             return ghost(zr0, (a,), p, 5, 16, 0)
         if not 0 < p < 25:
             return jnp.zeros((48, 128), F32)
-        at = 64 * a + (8 * q if b == 2 else 32 + 8 * (q - 12))
-        return place(rotate(zs0[1, b], -at, 1), rotate(zs0[0, b], 120 - at, 1), 0)
+        return place(zs0[1, b], zs0[0, b], 8 * a + (q if b == 2 else 4 + q - 12), 0)
 
     lane_r, lane_c = iota((128, 128), 0), iota((128, 128), 1)
     halve1 = jnp.where((lane_r // 2 == lane_c), 0.125, 0.0)
@@ -428,22 +429,20 @@
     next(k_gather)
     slabs(fk1, fk1, 7, 8, 6, 16, (1,), 2)
     edges(s["zk1"], s["zrk1"], 16, (), 3)
-    for off in wide:
-        push(rk2.at[2, 1, 1], rk2.at[2 - off[0], 1 - off[1], 1 - off[2]], 16, off)
     myz0 = inside_yz(48, 32, 128, 192, 256)
     row48 = iota((48, 128), 0)
     for p in range(26):
-        for a in range(2):
-            g = ghost0(a, p)
-            if a == 1:
-                sx = inside_x(p, 5, 16)
-                main = fk0[1, 0, p] * (myz0[:, 0:128] * sx)
-                if not 0 < p < 25:
-                    main = jnp.where((row48 >= 8) & (row48 < 40), main, 0.0)
-                fk0[1, 0, p] = main
-                g = g * (myz0[:, 128:256] * sx)
-            fk0[a, 1, p] = g
+        sx = inside_x(p, 5, 16)
+        main = fk0[1, 0, p] * (myz0[:, 0:128] * sx)
+        if not 0 < p < 25:
+            main = jnp.where((row48 >= 8) & (row48 < 40), main, 0.0)
+        fk0[1, 0, p] = main
+        fk0[1, 1, p] = ghost0(1, p) * (myz0[:, 128:256] * sx)
     l0.prepare(1, 13)
+    wait(recv, 20)
+    wait(recv, 21)
+    for p in range(1, 25):
+        fk0[0, 1, p] = ghost0(0, p)
     l0.sources(1, 13)
     l0.half("b", l0.v["b"], 1, 13)
     l0.sweep(l0.v["b"], (2, 12), (2, 12))
@@ -454,6 +453,8 @@
     slabs(fk1, fk1, 7, 8, 5, 16, (0,), 4)
     pack(lambda p: fk1[0, 7 + p, 8:24, :], s["zf1"], 8, 64)
     edges(s["zf1"], s["zrf1"], 16, (), 5)
+    for off in wide:
+        push(rk2.at[2, 1, 1], rk2.at[2 - off[0], 1 - off[1], 1 - off[2]], 16, off)
     wait(recv, 2)
     wait(recv, 3)
     wait(send, 2)
@@ -476,15 +477,6 @@
     in_y = ((row24 >= 8) | (iy > 0)) & ((row24 < 16) | (iy < N - 1))
     in_z = (lane24 < 32) | ((lane24 < 64) & (iz < N - 1)) | ((lane24 >= 96) & (iz > 0))
     myz2 = jnp.where(in_y & in_z, 1.0, 0.0)
-    wait(recv, 16)
-    for p in range(20):
-        b, q = divmod(p, 4)
-        sx = [flag(ix > 1), flag(ix > 0), 1.0, flag(ix < N - 1), flag(ix < N - 2)][b]
-        for by in range(3):
-            v = unpack2(lambda i, j, k: rk2[i, j, k], b, q, by)
-            fk2[1, 1 + p, 8 * by : 8 * by + 8, :] = v * (myz2[8 * by : 8 * by + 8] * sx)
-    l2.prepare(1, 11)
-
     wait(recv, 4)
     wait(recv, 5)
     wait(send, 4)
@@ -508,6 +500,15 @@
                 for by in range(3):
                     fk2[0, 1 + p, 8 * by : 8 * by + 8, :] = unpack2(lambda i, j, k: rf2[i, j, k], b, p % 4, by)
             l2.sources(1 + 2 * b, 3 + 2 * b)
+
+    wait(recv, 16)
+    for p in range(20):
+        b, q = divmod(p, 4)
+        sx = [flag(ix > 1), flag(ix > 0), 1.0, flag(ix < N - 1), flag(ix < N - 2)][b]
+        for by in range(3):
+            v = unpack2(lambda i, j, k: rk2[i, j, k], b, q, by)
+            fk2[1, 1 + p, 8 * by : 8 * by + 8, :] = v * (myz2[8 * by : 8 * by + 8] * sx)
+    l2.prepare(1, 11)
 
     wait(recv, 6)
     next(k_gather)
@@ -738,8 +739,8 @@
     shapes["up0"] = vmem(2, 12, 32, 128)
     shapes["up1"], shapes["tall1"] = vmem(10, 24, 128), vmem(10, 32, 128)
     shapes["dummy"] = vmem(256, 8, 128)
-    shapes["send"] = pltpu.SemaphoreType.DMA((20,))
-    shapes["recv"] = pltpu.SemaphoreType.DMA((20,))
+    shapes["send"] = pltpu.SemaphoreType.DMA((22,))
+    shapes["recv"] = pltpu.SemaphoreType.DMA((22,))
     shapes["load"] = pltpu.SemaphoreType.DMA((2,))
     return shapes
 

time: 67.8 us -> 64.4 us (0.950)
  Pallas kernels: 66.9 us -> 63.5 us
    pallas_call x1, Pallas kernels: 66.9 us -> 63.5 us  [on_device(): pl.pallas_call(kernel, out_shape=jax.ShapeDtypeStruct((16, 32, 128), F32)...]
where the time goes in v4:
time: 64.4 us; the launch traced here: 64.2 us
  Pallas kernels  63.5 us (99%)
  local copies, waits for them, and re-layouts  0.71 us (1%)
    pallas_call x1, Pallas kernels, on_device(): pl.pallas_call(kernel, out_shape=jax.ShapeDtypeStruct((16, 32, 128), F32)...  63.5 us

profile of v4, /device:TPU:1, one launch (start us, length us, event | category | flops | bytes accessed | tf_op | source)
XLA Modules:
  0.0 64.2 jit_solution(2664360100892742593)
XLA Ops:
  0.0 63.5 %vcycle.1 = f32[16,32,128]{2,1,0:T(8,128)S(1)} custom-call(f32[16,32,128]{2,1,0:T(8,128)} %f_hbm.1, f32[16,32,128]{2,1,0:T(8,128)} %k_hbm.1), custom_call_target="tpu_custom_call" | custom-call | tf_op jit(solution)/shard_map/vcycle/pallas_call | solution.py:752
  63.5 0.7 %copy.4 = f32[16,32,128]{2,1,0:T(8,128)} copy(f32[16,32,128]{2,1,0:T(8,128)S(1)} %vcycle.1) | data formatting | bytes 524288

commit v5 on v4

--- a/solution.py
+++ b/solution.py
@@ -94,12 +94,15 @@
 
     def prepare(self, lo, hi):
         shape = (self.rows, self.lanes)
-        hs = 0.5 * self.scale
+        hs = self.scale
+
+        def times(a):
+            return a if hs == 1.0 else hs * a
 
         def one(before, k, after):
             kyl, kyu = self.shift(k, 1), self.shift(k, -1)
             kzl, kzu = rotate(k, 1, 1), rotate(k, -1, 1)
-            wy, wz = hs * (k + kyl), hs * (k + kzl)
+            wy, wz = times(k + kyl), times(k + kzl)
             if self.closed:
                 row, lane = iota(shape, 0), iota(shape, 1)
                 kyl = jnp.where(row == 0, 0.0, kyl)
@@ -108,7 +111,7 @@
                 kzu = jnp.where(lane == self.lanes - 1, 0.0, kzu)
                 wy = jnp.where(row == 0, 0.0, wy)
                 wz = jnp.where(lane == 0, 0.0, wz)
-            diag = hs * (6.0 * k + before + after + kyl + kyu + kzl + kzu)
+            diag = times(6.0 * k + before + after + kyl + kyu + kzl + kzu)
             inside = k > 0.0
             inv = jnp.where(inside, 1.0 / jnp.where(inside, diag, 1.0), 0.0)
             return wy, wz, inv, diag
@@ -117,9 +120,9 @@
             even = self.even()
             k = [self.read(self.k, 2 * j - 2 + n) for n in range(4)]
             first, second = one(k[0], k[1], k[2]), one(k[1], k[2], k[3])
-            below = hs * (k[0] + k[1])
-            above = hs * (k[2] + k[3])
-            self.xin[j] = hs * (k[1] + k[2])
+            below = times(k[0] + k[1])
+            above = times(k[2] + k[3])
+            self.xin[j] = times(k[1] + k[2])
             self.xo["r"][j] = jnp.where(even, below, above)
             self.xo["b"][j] = jnp.where(even, above, below)
             for ref, n in ((self.y, 0), (self.z, 1), (self.i, 2)):
@@ -134,6 +137,7 @@
         def body(j):
             even = self.even()
             a, b = self.read(self.f, 2 * j - 1), self.read(self.f, 2 * j)
+            a, b = a + a, b + b
             red = jnp.where(even, a, b)
             self.g["r"][j] = red
             self.g["b"][j] = jnp.where(even, b, a)
@@ -225,8 +229,8 @@
 
     own0 = [fk0.at[a, 0, pl.ds(5, 16), pl.ds(8, 32)] for a in range(2)]
     loads = [pltpu.make_async_copy(r, own0[a], s["load"].at[a]) for a, r in enumerate((f_hbm, k_hbm))]
-    for c in loads:
-        c.start()
+    loads[1].start()
+    loads[0].start()
     near = [(a, b, c) for a in (-1, 0, 1) for b in (-1, 0, 1) for c in (-1, 0, 1) if (a, b, c) != (0, 0, 0)]
     wide = [(a, b, c) for a in (-2, -1, 0, 1, 2) for b in (-1, 0, 1) for c in (-1, 0, 1) if (a, b, c) != (0, 0, 0)]
     lines = []
@@ -237,8 +241,7 @@
     barrier = pltpu.get_barrier_semaphore()
     for off in partners:
         pl.semaphore_signal(barrier, inc=1, device_id=device(off), device_id_type=MESH)
-    for c in loads:
-        c.wait()
+    loads[1].wait()
     pl.semaphore_wait(barrier, len(partners))
 
     def pack(own, zp, planes, length):
@@ -299,6 +302,7 @@
     slabs(fk0, fk0, 5, 16, 4, 32, (1, 0), 0)
     for sx, a, b in ((1, 16, 0), (-1, 9, 25)):
         push(fk0.at[1, 0, a, pl.ds(8, 32)], fk0.at[1, 0, b, pl.ds(8, 32)], 0, (sx, 0, 0))
+    loads[0].wait()
     for a in (1, 0):
         pack(lambda p, a=a: fk0[a, 0, 5 + p, 8:40, :], zp0.at[:, a], 16, 128)
     lane32 = iota((32, 128), 1)
@@ -327,12 +331,12 @@
     pairk = s["pairk"]
     pair0, pair1, pair2, pair3 = s["pair0"], s["pair1"], s["pair2"], s["pair3"]
 
-    def coarse1(rows):
-        return spread(rows, halve1).reshape(8, 16, 128)
-
-    def coarse2():
+    def coarse1(rows, part):
+        return spread(rows, part * halve1).reshape(8, 16, 128)
+
+    def coarse2(part):
         flat = pair1.reshape(64, 128)
-        return spread(row_pairs(flat, 32), halve2).reshape(4, 8, 128)
+        return spread(row_pairs(flat, 32), part * halve2).reshape(4, 8, 128)
 
     def packed2(value):
         total = value[0]
@@ -342,14 +346,14 @@
 
     row8, col8 = iota((8, 8), 0), iota((8, 8), 1)
 
-    def coarse3():
-        place_rows = jnp.where(row8 == 4 * lax.rem(iy, 2) + col8 // 2, 1.0, 0.0)
+    def coarse3(part):
+        place_rows = jnp.where(row8 == 4 * (ix // 4) + col8 // 2, 1.0, 0.0)
         total = None
         for dx in range(2):
             group = lax.rem(2 * ix + dx, 8)
-            into = jnp.where((lane_r < 32) & (lane_c == 16 * group + lane_r // 2), 0.125, 0.0)
-            part = spread(select_rows(place_rows, pair2[dx]), into)
-            total = part if total is None else total + part
+            into = jnp.where((lane_r < 32) & (lane_c == 16 * group + lane_r // 2), 0.125 * part, 0.0)
+            piece = spread(select_rows(place_rows, pair2[dx]), into)
+            total = piece if total is None else total + piece
         return total
 
     def gather(tile, g1, g2, g3, sem):
@@ -358,15 +362,15 @@
             push(g1.at[ix], g1.at[ix], sem, (d, 0, 0))
         yield
         wait(recv, sem)
-        g2[iy, 0] = g1[0] + g1[1] + g1[2] + g1[3]
-        g2[iy, 1] = g1[4] + g1[5] + g1[6] + g1[7]
+        g2[iy] = (g1[0] + g1[1]) + (g1[2] + g1[3]) + ((g1[4] + g1[5]) + (g1[6] + g1[7]))
         for d in range(1, N):
             push(g2.at[iy], g2.at[iy], sem + 1, (0, d, 0))
         yield
         wait(recv, sem + 1)
         for o in range(4):
-            for h in range(2):
-                g3[iz, h, o] = g2[2 * o, h] + g2[2 * o + 1, h]
+            a, b = g2[2 * o], g2[2 * o + 1]
+            g3[iz, 0, o] = jnp.where(iota((8, 128), 0) < 4, a, rotate(b, 4, 0))
+            g3[iz, 1, o] = jnp.where(iota((8, 128), 0) < 4, rotate(a, 4, 0), b)
         for d in range(1, N):
             push(g3.at[iz], g3.at[iz], sem + 2, (0, 0, d))
         yield
@@ -389,16 +393,16 @@
 
     for i in range(8):
         pairk[i] = fk0[1, 0, 5 + 2 * i, 8:40, :] + fk0[1, 0, 6 + 2 * i, 8:40, :]
-    k1_own = coarse1(row_pairs(pairk.reshape(256, 128), 128))
+    k1_own = coarse1(row_pairs(pairk.reshape(256, 128), 128), 1.0)
     fk1[1, 7:15, 8:24, :] = k1_own
     for i in range(4):
         pair1[i] = k1_own[2 * i] + k1_own[2 * i + 1]
-    k2_own = coarse2()
+    k2_own = coarse2(1.0)
     rk2 = s["rk2"]
-    rk2[2, 1, 1] = packed2(k2_own)
+    rk2[1, 1, 2] = packed2(k2_own)
     for i in range(2):
         pair2[i] = k2_own[2 * i] + k2_own[2 * i + 1]
-    k_gather = gather(coarse3(), s["gk1"], s["gk2"], s["gk3"], 10)
+    k_gather = gather(coarse3(1.0), s["gk1"], s["gk2"], s["gk3"], 10)
     pack(lambda p: fk1[1, 7 + p, 8:24, :], s["zk1"], 8, 64)
 
     for lev, last in ((l0, 13), (l1, 11), (l2, 11), (l3, 9)):
@@ -427,6 +431,8 @@
     wait(recv, 1)
     wait(send, 0)
     next(k_gather)
+    for sx in (-2, -1, 1, 2):
+        push(rk2.at[1, 1, 2], rk2.at[1, 1, 2 - sx], 16, (sx, 0, 0))
     slabs(fk1, fk1, 7, 8, 6, 16, (1,), 2)
     edges(s["zk1"], s["zrk1"], 16, (), 3)
     myz0 = inside_yz(48, 32, 128, 192, 256)
@@ -447,14 +453,15 @@
     l0.half("b", l0.v["b"], 1, 13)
     l0.sweep(l0.v["b"], (2, 12), (2, 12))
     l0.residual(3, 11, (8, 40), pair0)
-    f1_own = coarse1(pair0[:, 4:20, :].reshape(128, 128))
+    f1_own = coarse1(pair0[:, 4:20, :].reshape(128, 128), 0.5)
     fk1[0, 7:15, 8:24, :] = f1_own
 
     slabs(fk1, fk1, 7, 8, 5, 16, (0,), 4)
     pack(lambda p: fk1[0, 7 + p, 8:24, :], s["zf1"], 8, 64)
     edges(s["zf1"], s["zrf1"], 16, (), 5)
-    for off in wide:
-        push(rk2.at[2, 1, 1], rk2.at[2 - off[0], 1 - off[1], 1 - off[2]], 16, off)
+    wait(recv, 16)
+    for sy in (-1, 1):
+        push(rk2.at[1, 1], rk2.at[1, 1 - sy], 22, (0, sy, 0))
     wait(recv, 2)
     wait(recv, 3)
     wait(send, 2)
@@ -463,6 +470,9 @@
         v = jnp.where(lane32 < 64, fk1[1, p], ghost(s["zrk1"], (), p, 7, 8, 64))
         fk1[1, p] = v * (myz1 * inside_x(p, 7, 8))
     l1.prepare(1, 11)
+    wait(recv, 22)
+    for sz in (-1, 1):
+        push(rk2.at[1], rk2.at[1 - sz], 23, (0, 0, sz))
     next(k_gather)
 
     lane8 = iota((8, 128), 1)
@@ -487,7 +497,7 @@
     l1.sweep(l1.v["b"], (3, 9), (3, 9))
     l1.residual(4, 8, (8, 24), pair1)
     rf2 = s["rf2"]
-    rf2[2, 1, 1] = packed2(coarse2())
+    rf2[2, 1, 1] = packed2(coarse2(0.5))
 
     far = [off for off in wide if off not in near]
     for sem, group in ((6, near), (19, far)):
@@ -501,12 +511,12 @@
                     fk2[0, 1 + p, 8 * by : 8 * by + 8, :] = unpack2(lambda i, j, k: rf2[i, j, k], b, p % 4, by)
             l2.sources(1 + 2 * b, 3 + 2 * b)
 
-    wait(recv, 16)
+    wait(recv, 23)
     for p in range(20):
         b, q = divmod(p, 4)
         sx = [flag(ix > 1), flag(ix > 0), 1.0, flag(ix < N - 1), flag(ix < N - 2)][b]
         for by in range(3):
-            v = unpack2(lambda i, j, k: rk2[i, j, k], b, q, by)
+            v = unpack2(lambda i, j, k: rk2[k, j, i], b, q, by)
             fk2[1, 1 + p, 8 * by : 8 * by + 8, :] = v * (myz2[8 * by : 8 * by + 8] * sx)
     l2.prepare(1, 11)
 
@@ -516,7 +526,7 @@
     l2.half("b", l2.v["b"], 3, 9)
     l2.sweep(l2.v["b"], (4, 8), (4, 8))
     l2.residual(5, 7, (8, 16), pair2)
-    f_gather = gather(coarse3(), s["gf1"], s["gf2"], s["gf3"], 13)
+    f_gather = gather(coarse3(0.5), s["gf1"], s["gf2"], s["gf3"], 13)
     next(f_gather)
     slabs(l1.v["b"], s["v1"], 4, 4, 3, 16, (), 7)
     pack(lambda p: l1.v["b"][4 + p, 8:24, :], s["zpu1"], 4, 64)
@@ -545,18 +555,18 @@
         push(ru2.at[2, 1, 1], ru2.at[2 - off[0], 1 - off[1], 1 - off[2]], 9, off)
     pair3_flat = pair3.reshape(8 * 32, 128)
 
-    def coarse4():
+    def coarse4(part):
         rows = row_pairs(pair3_flat, 128).reshape(8, 16, 128)
         out = None
         for h in range(2):
-            into = jnp.where(lane_c == 64 * h + lane_r // 2, 0.125, 0.0)
-            part = spread(rows[4 * h : 4 * h + 4].reshape(64, 128), into)
-            out = part if out is None else out + part
+            into = jnp.where(lane_c == 64 * h + lane_r // 2, 0.125 * part, 0.0)
+            piece = spread(rows[4 * h : 4 * h + 4].reshape(64, 128), into)
+            out = piece if out is None else out + piece
         return out.reshape(4, 16, 128)
 
     for i in range(8):
         pair3[i] = fk3[1, 1 + 2 * i] + fk3[1, 2 + 2 * i]
-    k4 = coarse4()
+    k4 = coarse4(1.0)
     shape4 = (4, 16, 128)
     row4, lane4 = iota(shape4, 1), iota(shape4, 2)
     z4 = lane4 & 63
@@ -602,7 +612,7 @@
     l3.half("b", l3.v["b"], 1, 9)
     l3.sweep(l3.v["b"], (1, 9), (1, 9))
     l3.residual(1, 9, (0, 32), pair3)
-    f4 = coarse4()
+    f4 = coarse4(0.5)
     w4[8] = f4
 
     def around4(v):
@@ -725,11 +735,12 @@
         shapes["z" + name] = vmem(2, 16, 128)
     for name in ("zrk1", "zrf1", "zru1"):
         shapes[name] = vmem(2, 3, 32, 128)
-    for name in ("rk2", "rf2", "ru2"):
+    for name in ("rf2", "ru2"):
         shapes[name] = vmem(5, 3, 3, 8, 128)
+    shapes["rk2"] = vmem(3, 3, 5, 8, 128)
     for name in "kf":
         shapes[f"g{name}1"] = vmem(8, 8, 128)
-        shapes[f"g{name}2"] = vmem(8, 2, 8, 128)
+        shapes[f"g{name}2"] = vmem(8, 8, 128)
         shapes[f"g{name}3"] = vmem(8, 2, 4, 8, 128)
     shapes["pair0"], shapes["pair1"] = vmem(8, 24, 128), vmem(4, 16, 128)
     shapes["pairk"], shapes["outn"] = vmem(8, 32, 128), vmem(16, 48, 128)
@@ -739,8 +750,8 @@
     shapes["up0"] = vmem(2, 12, 32, 128)
     shapes["up1"], shapes["tall1"] = vmem(10, 24, 128), vmem(10, 32, 128)
     shapes["dummy"] = vmem(256, 8, 128)
-    shapes["send"] = pltpu.SemaphoreType.DMA((22,))
-    shapes["recv"] = pltpu.SemaphoreType.DMA((22,))
+    shapes["send"] = pltpu.SemaphoreType.DMA((24,))
+    shapes["recv"] = pltpu.SemaphoreType.DMA((24,))
     shapes["load"] = pltpu.SemaphoreType.DMA((2,))
     return shapes
 

time: 64.4 us -> 63 us (0.978)
  Pallas kernels: 63.5 us -> 62.1 us
    pallas_call x1, Pallas kernels: 63.5 us -> 62.1 us  [on_device(): pl.pallas_call(kernel, out_shape=jax.ShapeDtypeStruct((16, 32, 128), F32)...]
where the time goes in v5:
time: 63 us; the launch traced here: 62.8 us
  Pallas kernels  62.1 us (99%)
  local copies, waits for them, and re-layouts  0.71 us (1%)
    pallas_call x1, Pallas kernels, on_device(): pl.pallas_call(kernel, out_shape=jax.ShapeDtypeStruct((16, 32, 128), F32)...  62.1 us

profile of v5, /device:TPU:1, one launch (start us, length us, event | category | flops | bytes accessed | tf_op | source)
XLA Modules:
  0.0 62.8 jit_solution(8286722666552802191)
XLA Ops:
  0.0 62.1 %vcycle.1 = f32[16,32,128]{2,1,0:T(8,128)S(1)} custom-call(f32[16,32,128]{2,1,0:T(8,128)} %f_hbm.1, f32[16,32,128]{2,1,0:T(8,128)} %k_hbm.1), custom_call_target="tpu_custom_call" | custom-call | tf_op jit(solution)/shard_map/vcycle/pallas_call | solution.py:763
  62.1 0.7 %copy.4 = f32[16,32,128]{2,1,0:T(8,128)} copy(f32[16,32,128]{2,1,0:T(8,128)S(1)} %vcycle.1) | data formatting | bytes 524288

commit v6 on v5

--- a/solution.py
+++ b/solution.py
@@ -233,11 +233,7 @@
     loads[0].start()
     near = [(a, b, c) for a in (-1, 0, 1) for b in (-1, 0, 1) for c in (-1, 0, 1) if (a, b, c) != (0, 0, 0)]
     wide = [(a, b, c) for a in (-2, -1, 0, 1, 2) for b in (-1, 0, 1) for c in (-1, 0, 1) if (a, b, c) != (0, 0, 0)]
-    lines = []
-    for a in range(3):
-        for d in range(1, N):
-            lines.append(tuple((d if d <= 4 else d - N) if b == a else 0 for b in range(3)))
-    partners = wide + [o for o in lines if o not in wide]
+    partners = near + [(d, 0, 0) for d in (-3, -2, 2, 3, 4)]
     barrier = pltpu.get_barrier_semaphore()
     for off in partners:
         pl.semaphore_signal(barrier, inc=1, device_id=device(off), device_id_type=MESH)
@@ -302,16 +298,16 @@
     slabs(fk0, fk0, 5, 16, 4, 32, (1, 0), 0)
     for sx, a, b in ((1, 16, 0), (-1, 9, 25)):
         push(fk0.at[1, 0, a, pl.ds(8, 32)], fk0.at[1, 0, b, pl.ds(8, 32)], 0, (sx, 0, 0))
+    pack(lambda p: fk0[1, 0, 5 + p, 8:40, :], zp0.at[:, 1], 16, 128)
+    edges(zp0, zr0, 32, (1,), 1, (0,))
     loads[0].wait()
-    for a in (1, 0):
-        pack(lambda p, a=a: fk0[a, 0, 5 + p, 8:40, :], zp0.at[:, a], 16, 128)
+    pack(lambda p: fk0[0, 0, 5 + p, 8:40, :], zp0.at[:, 0], 16, 128)
     lane32 = iota((32, 128), 1)
     for side in range(2):
         fs, ks = [rotate(zp0[side, a], 8 * side, 1) for a in range(2)]
         v = jnp.where(lane32 < 32, fs, rotate(fs, -64, 1))
         v = jnp.where(lane32 < 64, v, jnp.where(lane32 < 96, rotate(ks, 64, 1), ks))
         ze0[side] = rotate(v, -8 * side, 1)
-    edges(zp0, zr0, 32, (1,), 1, (0,))
     edges(ze0, zs0, 32, (), 1, (-1, 1))
     slabs(fk0, fk0, 5, 16, 4, 32, (0, 0), 20)
     edges(zp0, zr0, 32, (0,), 21, (0,))
@@ -473,7 +469,6 @@
     wait(recv, 22)
     for sz in (-1, 1):
         push(rk2.at[1], rk2.at[1 - sz], 23, (0, 0, sz))
-    next(k_gather)
 
     lane8 = iota((8, 128), 1)
 
@@ -528,6 +523,11 @@
     l2.residual(5, 7, (8, 16), pair2)
     f_gather = gather(coarse3(0.5), s["gf1"], s["gf2"], s["gf3"], 13)
     next(f_gather)
+    ru2 = s["ru2"]
+    total = jnp.where(lane8 < 32, l2.v["b"][5, 8:16, :], 0.0)
+    ru2[1, 1, 2] = total + rotate(jnp.where(lane8 < 32, l2.v["b"][6, 8:16, :], 0.0), 32, 1)
+    for sx in (-2, -1, 1, 2):
+        push(ru2.at[1, 1, 2], ru2.at[1, 1, 2 - sx], 9, (sx, 0, 0))
     slabs(l1.v["b"], s["v1"], 4, 4, 3, 16, (), 7)
     pack(lambda p: l1.v["b"][4 + p, 8:24, :], s["zpu1"], 4, 64)
     edges(s["zpu1"], s["zru1"], 16, (), 8)
@@ -539,20 +539,22 @@
     pack(lambda p: vb0n[3 + p, 8:40, :], s["zpu0"], 8, 128)
     v0n[0, 3:11, 8:40, :] = vb0n[3:11, 8:40, :]
     next(f_gather)
+    wait(recv, 9)
+    for sy in (-1, 1):
+        push(ru2.at[1, 1], ru2.at[1, 1 - sy], 24, (0, sy, 0))
     slabs(vb0n, v0n.at[0], 3, 8, 2, 32, (), 17)
     edges(s["zpu0"], s["zru0"], 32, (), 18)
     wait(recv, 19)
     source2((0, 4))
+    next(k_gather)
+    next(f_gather)
+    wait(recv, 24)
+    for sz in (-1, 1):
+        push(ru2.at[1], ru2.at[1 - sz], 25, (0, 0, sz))
     for _ in k_gather:
         pass
     unpack3(s["gk3"], fk3.at[1])
     l3.prepare(1, 9)
-    next(f_gather)
-    ru2 = s["ru2"]
-    total = jnp.where(lane8 < 32, l2.v["b"][5, 8:16, :], 0.0)
-    ru2[2, 1, 1] = total + rotate(jnp.where(lane8 < 32, l2.v["b"][6, 8:16, :], 0.0), 32, 1)
-    for off in wide:
-        push(ru2.at[2, 1, 1], ru2.at[2 - off[0], 1 - off[1], 1 - off[2]], 9, off)
     pair3_flat = pair3.reshape(8 * 32, 128)
 
     def coarse4(part):
@@ -605,6 +607,24 @@
     w4[6] = jnp.where(odd4 == 0, inv4, 0.0)
     w4[7] = jnp.where(odd4 == 1, inv4, 0.0)
 
+    wait(recv, 7)
+    wait(recv, 8)
+    v1 = s["v1"]
+    for j in range(1, 11):
+        v1[j] = jnp.where(lane32 < 64, v1[j], ghost(s["zru1"], (), j, 4, 4, 64))
+    wait(recv, 17)
+    wait(recv, 18)
+    v0 = s["v0"]
+    for j in range(1, 13):
+        v0n[1, j] = ghost(s["zru0"], (), j, 3, 8, 0)
+    for j in range(1, 13):
+        v0[j] = l0.read(v0n, j)
+    wait(recv, 25)
+    v2 = s["v2"]
+    for j in range(1, 11):
+        b, q = divmod(j - 1, 2)
+        for by in range(3):
+            v2[j, 8 * by : 8 * by + 8, :] = unpack2(lambda i, j, k: ru2[k, j, i], b, q, by)
     for _ in f_gather:
         pass
     unpack3(s["gf3"], fk3.at[0])
@@ -643,7 +663,6 @@
     for j in range(1, 9):
         u3[2 + 2 * j], u3[3 + 2 * j] = l3.planes(v3, j)
 
-    v2 = s["v2"]
     zoff = jnp.where(lane_c < 64, lane_c, lane_c - 128)
     source_lane = 16 * iz + ((zoff + 128) // 2 - 64)
     spread_z = jnp.where((lane_r == source_lane) & ((lane_c < 64) | (lane_c >= 96)), 1.0, 0.0)
@@ -651,11 +670,7 @@
     stretched = spread(u3[pl.ds(2 * ix, 10)].reshape(320, 128), spread_z)
     side_by_side = jnp.concatenate([stretched[32 * j : 32 * j + 32] for j in range(10)], axis=1)
     corr2 = select_rows(spread_y, side_by_side)
-    wait(recv, 9)
     for j in range(1, 11):
-        b, q = divmod(j - 1, 2)
-        for by in range(3):
-            v2[j, 8 * by : 8 * by + 8, :] = unpack2(lambda i, j, k: ru2[i, j, k], b, q, by)
         l2.correct(v2, j, corr2[:, 128 * (j - 1) : 128 * j])
     l2.sweep(v2, (2, 10), (2, 10))
     l2.sweep(v2, (3, 9), (3, 9))
@@ -667,11 +682,7 @@
         coarse += list(l2.planes(v2, j))
     up1[...] = spread(jnp.concatenate(coarse[1:11], axis=0), spread1).reshape(10, 24, 128)
     tall1 = s["tall1"]
-    wait(recv, 7)
-    wait(recv, 8)
-    v1 = s["v1"]
     for j in range(1, 11):
-        v1[j] = jnp.where(lane32 < 64, v1[j], ghost(s["zru1"], (), j, 4, 4, 64))
         part = up1[j - 1, 4:20, :]
         tall1[j - 1, pl.ds(0, 16, 2), :] = part
         tall1[j - 1, pl.ds(1, 16, 2), :] = part
@@ -686,18 +697,13 @@
         coarse += list(l1.planes(v1, j))
     wide0 = spread(jnp.concatenate(coarse, axis=0), spread0).reshape(12, 32, 256)
     up0[0], up0[1] = wide0[:, :, 0:128], wide0[:, :, 128:256]
-    wait(recv, 17)
-    wait(recv, 18)
-    v0 = s["v0"]
-    for j in range(1, 13):
-        v0n[1, j] = ghost(s["zru0"], (), j, 3, 8, 0)
     for j in range(1, 13):
         tiles = []
         for t in range(2):
             rows = [up0[t, j - 1, pl.ds(4 + c, 8, 3), :] for c in range(3)]
             tiles.append(jnp.concatenate([rows[c // 2] for c in range(6)], axis=0))
         corr = jnp.concatenate(tiles, axis=1)
-        v0[j] = jnp.where(l0.i["b"][j] > 0.0, l0.read(v0n, j) + corr, 0.0)
+        v0[j] = jnp.where(l0.i["b"][j] > 0.0, v0[j] + corr, 0.0)
     l0.sweep(v0, (1, 13), (2, 12))
     l0.half("r", v0, 2, 12)
     outn = s["outn"]
@@ -735,9 +741,9 @@
         shapes["z" + name] = vmem(2, 16, 128)
     for name in ("zrk1", "zrf1", "zru1"):
         shapes[name] = vmem(2, 3, 32, 128)
-    for name in ("rf2", "ru2"):
-        shapes[name] = vmem(5, 3, 3, 8, 128)
-    shapes["rk2"] = vmem(3, 3, 5, 8, 128)
+    shapes["rf2"] = vmem(5, 3, 3, 8, 128)
+    for name in ("rk2", "ru2"):
+        shapes[name] = vmem(3, 3, 5, 8, 128)
     for name in "kf":
         shapes[f"g{name}1"] = vmem(8, 8, 128)
         shapes[f"g{name}2"] = vmem(8, 8, 128)
@@ -750,8 +756,8 @@
     shapes["up0"] = vmem(2, 12, 32, 128)
     shapes["up1"], shapes["tall1"] = vmem(10, 24, 128), vmem(10, 32, 128)
     shapes["dummy"] = vmem(256, 8, 128)
-    shapes["send"] = pltpu.SemaphoreType.DMA((24,))
-    shapes["recv"] = pltpu.SemaphoreType.DMA((24,))
+    shapes["send"] = pltpu.SemaphoreType.DMA((26,))
+    shapes["recv"] = pltpu.SemaphoreType.DMA((26,))
     shapes["load"] = pltpu.SemaphoreType.DMA((2,))
     return shapes
 

time: 63 us -> 62.2 us (0.987)
  Pallas kernels: 62.1 us -> 61.4 us
    pallas_call x1, Pallas kernels: 62.1 us -> 61.4 us  [on_device(): pl.pallas_call(kernel, out_shape=jax.ShapeDtypeStruct((16, 32, 128), F32)...]
where the time goes in v6:
time: 62.2 us; the launch traced here: 62.1 us
  Pallas kernels  61.4 us (99%)
  local copies, waits for them, and re-layouts  0.71 us (1%)
    pallas_call x1, Pallas kernels, on_device(): pl.pallas_call(kernel, out_shape=jax.ShapeDtypeStruct((16, 32, 128), F32)...  61.4 us

profile of v6, /device:TPU:1, one launch (start us, length us, event | category | flops | bytes accessed | tf_op | source)
XLA Modules:
  0.0 62.1 jit_solution(2574132118045018783)
XLA Ops:
  0.0 61.4 %vcycle.1 = f32[16,32,128]{2,1,0:T(8,128)S(1)} custom-call(f32[16,32,128]{2,1,0:T(8,128)} %f_hbm.1, f32[16,32,128]{2,1,0:T(8,128)} %k_hbm.1), custom_call_target="tpu_custom_call" | custom-call | tf_op jit(solution)/shard_map/vcycle/pallas_call | solution.py:769
  61.4 0.7 %copy.4 = f32[16,32,128]{2,1,0:T(8,128)} copy(f32[16,32,128]{2,1,0:T(8,128)S(1)} %vcycle.1) | data formatting | bytes 524288

commit v7 on v6

--- a/solution.py
+++ b/solution.py
@@ -619,12 +619,6 @@
         v0n[1, j] = ghost(s["zru0"], (), j, 3, 8, 0)
     for j in range(1, 13):
         v0[j] = l0.read(v0n, j)
-    wait(recv, 25)
-    v2 = s["v2"]
-    for j in range(1, 11):
-        b, q = divmod(j - 1, 2)
-        for by in range(3):
-            v2[j, 8 * by : 8 * by + 8, :] = unpack2(lambda i, j, k: ru2[k, j, i], b, q, by)
     for _ in f_gather:
         pass
     unpack3(s["gf3"], fk3.at[0])
@@ -663,6 +657,12 @@
     for j in range(1, 9):
         u3[2 + 2 * j], u3[3 + 2 * j] = l3.planes(v3, j)
 
+    wait(recv, 25)
+    v2 = s["v2"]
+    for j in range(1, 11):
+        b, q = divmod(j - 1, 2)
+        for by in range(3):
+            v2[j, 8 * by : 8 * by + 8, :] = unpack2(lambda i, j, k: ru2[k, j, i], b, q, by)
     zoff = jnp.where(lane_c < 64, lane_c, lane_c - 128)
     source_lane = 16 * iz + ((zoff + 128) // 2 - 64)
     spread_z = jnp.where((lane_r == source_lane) & ((lane_c < 64) | (lane_c >= 96)), 1.0, 0.0)

time: 62.2 us -> 62.3 us (level)
  no operation moved by 1% of the time
where the time goes in v7:
time: 62.3 us; the launch traced here: 62.1 us
  Pallas kernels  61.4 us (99%)
  local copies, waits for them, and re-layouts  0.71 us (1%)
    pallas_call x1, Pallas kernels, on_device(): pl.pallas_call(kernel, out_shape=jax.ShapeDtypeStruct((16, 32, 128), F32)...  61.4 us

profile of v7, /device:TPU:1, one launch (start us, length us, event | category | flops | bytes accessed | tf_op | source)
XLA Modules:
  0.0 62.1 jit_solution(1412024808773040164)
XLA Ops:
  0.0 61.4 %vcycle.1 = f32[16,32,128]{2,1,0:T(8,128)S(1)} custom-call(f32[16,32,128]{2,1,0:T(8,128)} %f_hbm.1, f32[16,32,128]{2,1,0:T(8,128)} %k_hbm.1), custom_call_target="tpu_custom_call" | custom-call | tf_op jit(solution)/shard_map/vcycle/pallas_call | solution.py:769
  61.4 0.7 %copy.4 = f32[16,32,128]{2,1,0:T(8,128)} copy(f32[16,32,128]{2,1,0:T(8,128)S(1)} %vcycle.1) | data formatting | bytes 524288

commit v8 on v6

--- a/solution.py
+++ b/solution.py
@@ -539,6 +539,7 @@
     pack(lambda p: vb0n[3 + p, 8:40, :], s["zpu0"], 8, 128)
     v0n[0, 3:11, 8:40, :] = vb0n[3:11, 8:40, :]
     next(f_gather)
+    next(k_gather)
     wait(recv, 9)
     for sy in (-1, 1):
         push(ru2.at[1, 1], ru2.at[1, 1 - sy], 24, (0, sy, 0))
@@ -546,7 +547,6 @@
     edges(s["zpu0"], s["zru0"], 32, (), 18)
     wait(recv, 19)
     source2((0, 4))
-    next(k_gather)
     next(f_gather)
     wait(recv, 24)
     for sz in (-1, 1):

time: 62.2 us -> 62.2 us (level)
  no operation moved by 1% of the time
where the time goes in v8:
time: 62.2 us; the launch traced here: 62.1 us
  Pallas kernels  61.4 us (99%)
  local copies, waits for them, and re-layouts  0.71 us (1%)
    pallas_call x1, Pallas kernels, on_device(): pl.pallas_call(kernel, out_shape=jax.ShapeDtypeStruct((16, 32, 128), F32)...  61.4 us

profile of v8, /device:TPU:1, one launch (start us, length us, event | category | flops | bytes accessed | tf_op | source)
XLA Modules:
  0.0 62.1 jit_solution(12818920697221741555)
XLA Ops:
  0.0 61.4 %vcycle.1 = f32[16,32,128]{2,1,0:T(8,128)S(1)} custom-call(f32[16,32,128]{2,1,0:T(8,128)} %f_hbm.1, f32[16,32,128]{2,1,0:T(8,128)} %k_hbm.1), custom_call_target="tpu_custom_call" | custom-call | tf_op jit(solution)/shard_map/vcycle/pallas_call | solution.py:769
  61.4 0.7 %copy.4 = f32[16,32,128]{2,1,0:T(8,128)} copy(f32[16,32,128]{2,1,0:T(8,128)S(1)} %vcycle.1) | data formatting | bytes 524288
